TPU v7x, 512 devices: a whole 4x4x16 slice. The times are simulated.
512 devices in a mesh: gz: 32 (over z, core), xy: 16 (over x, y).
Axes of the slice: x: 4, y: 4, z: 16, core: 2. Of those that a mesh axis runs over, the one named last changes fastest.
Arguments:
- fields: float32 [4, 128, 128, 1024], P(None, 'gz', 'xy'), may hold values from -6 to 6
- conductance: float32 [4, 128, 128, 1024], P(None, 'gz', 'xy'), may hold values from 1000 to 10000
- lateral: float32 [4], replicated, may hold values from 0.05 to 0.24
- partition: float32 [3], replicated, may hold values from 0.1 to 0.8
- arm_step: float32 [3, 64, 64], replicated, may hold values from -0.2 to 0.95
- profiles: float32 [3, 8192, 64, 128], P(None, ('gz', 'xy')), may hold values from -6 to 6
- tile_ids: int32 [512, 16], P(('gz', 'xy')), may hold values from 0 to 255, as said below
- tile_count: int32 [512], P(('gz', 'xy')), may hold values from 0 to 16, as said below
Outputs:
- new_fields: float32 [4, 128, 128, 1024], P(None, 'gz', 'xy')
- new_profiles: float32 [3, 8192, 64, 128], P(None, ('gz', 'xy'))
Inputs may be any that keep to these rules, and one draw needn't show every extreme that they name: `tile_ids`: the first tile_count entries of a device's row are distinct; an entry numbers a tile of that device's own block. `tile_count`: some device has exactly 16; the counts of two devices with the same gz index whose xy indices differ by 8 add up to at most 16.
All inputs are finite; a program needn't handle non-finite values.
Results may differ from a plain program's by a relative error of at most 0.0003.
Values sent between devices are 32-bit elements; how exact they have to be, the bound alone decides.
A program may use at most 64 MiB of HBM per device.

v0:
```python
import jax
import jax.numpy as jnp
from jax import lax
from jax.sharding import PartitionSpec as P

SUB = 16


def from_behind(block, axis, distance):
    devices = range(lax.axis_size(axis))
    route = [(i - distance, i) for i in devices if i - distance in devices]
    return lax.ppermute(block, axis, route)


def extended(cells, sides, width):
    for axis, dim in sides:
        count = lax.axis_size(axis)
        ends = count - 1
        head = lax.slice_in_dim(cells, 0, width, axis=dim)
        tail = lax.slice_in_dim(cells, cells.shape[dim] - width, cells.shape[dim], axis=dim)
        cells = jnp.concatenate(
            [
                lax.ppermute(tail, axis, [(i, (i + 1) % count) for i in range(ends)]),
                cells,
                lax.ppermute(head, axis, [((i + 1) % count, i) for i in range(ends)]),
            ],
            axis=dim,
        )
    return cells


def lever_update(cell_values, profile, partition, arm_step):
    solid_frac = 0.9 / (1.0 + jnp.exp(cell_values[3]))
    solute = cell_values[:3]

    def substep(step_at, current):
        fraction = solid_frac * ((step_at + 1).astype(current.dtype) / SUB)
        average = jnp.mean(current, axis=2)
        liquid = (solute - fraction * average) / (1.0 - fraction)
        spread = jnp.einsum("jab,jsbc->jsac", arm_step, current, precision=lax.Precision.HIGHEST)
        return spread.at[:, :, -1, :].add(0.5 * partition[:, None, None] * liquid)

    evolved = lax.fori_loop(0, SUB, substep, profile)
    change = solid_frac * (jnp.mean(evolved, axis=2) - partition[:, None, None] * solute)
    return (evolved, change)


def row_of(values, row_at):
    return values[..., row_at, :]


def eliminate(lower_c, middle_c, upper_c, source):
    height = middle_c.shape[-2]
    fwd_low = [None] * height
    fwd_up = [None] * height
    fwd_rhs = [None] * height
    fwd_low[1] = row_of(lower_c, 1) / row_of(middle_c, 1)
    fwd_up[1] = row_of(upper_c, 1) / row_of(middle_c, 1)
    fwd_rhs[1] = row_of(source, 1) / row_of(middle_c, 1)
    for row_at in range(2, height):
        factor = row_of(lower_c, row_at)
        pivot_value = row_of(middle_c, row_at) - factor * fwd_up[row_at - 1]
        fwd_low[row_at] = -factor * fwd_low[row_at - 1] / pivot_value
        fwd_up[row_at] = row_of(upper_c, row_at) / pivot_value
        fwd_rhs[row_at] = (row_of(source, row_at) - factor * fwd_rhs[row_at - 1]) / pivot_value
    back_first = list(fwd_low)
    back_last = list(fwd_up)
    back_rhs = list(fwd_rhs)
    row_at = 1
    ratio_up = fwd_up[row_at]
    back_first[row_at] = fwd_low[row_at] - ratio_up * back_first[row_at + 1]
    back_last[row_at] = -ratio_up * back_last[row_at + 1]
    back_rhs[row_at] = fwd_rhs[row_at] - ratio_up * back_rhs[row_at + 1]
    top_up = row_of(upper_c, 0)
    pivot_first = row_of(middle_c, 0) - top_up * back_first[1]
    first_row = jnp.stack(
        [
            row_of(lower_c, 0) / pivot_first,
            -top_up * back_last[1] / pivot_first,
            (row_of(source, 0) - top_up * back_rhs[1]) / pivot_first,
        ]
    )
    last_row = jnp.stack([fwd_low[height - 1], fwd_up[height - 1], fwd_rhs[height - 1]])
    return (first_row, last_row, (back_first, back_last, back_rhs))


def combine(current, below_rows, above_rows):
    pivot_value = 1.0 - current[0] * below_rows[1] - current[1] * above_rows[0]
    return jnp.stack(
        [
            -current[0] * below_rows[0] / pivot_value,
            -current[1] * above_rows[1] / pivot_value,
            (current[2] - current[0] * below_rows[2] - current[1] * above_rows[2]) / pivot_value,
        ]
    )


def reduced_solve(first_row, last_row, mover, blocks):
    below_rows = mover(last_row, 1)
    above_rows = mover(first_row, -1)
    first_row, last_row = (
        combine(first_row, below_rows, last_row),
        combine(last_row, first_row, above_rows),
    )
    stride = 1
    while stride < blocks:
        paired_rows = jnp.concatenate([first_row, last_row], axis=0)
        below_rows = mover(paired_rows, stride)
        above_rows = mover(paired_rows, -stride)
        first_row, last_row = (
            combine(first_row, below_rows[:3], above_rows[:3]),
            combine(last_row, below_rows[3:], above_rows[3:]),
        )
        stride = stride * 2
    return (first_row[2], last_row[2])


def assemble(first_value, last_value, interior):
    back_first, back_last, back_rhs = interior
    height = len(back_rhs)
    planes = [first_value]
    for row_at in range(1, height - 1):
        planes.append(
            back_rhs[row_at] - back_first[row_at] * first_value - back_last[row_at] * last_value
        )
    planes.append(last_value)
    return jnp.stack(planes, axis=-2)


def shift_rows(stacked, offset):
    return from_behind(stacked, "gz", offset)


def body(fields, conductance, lateral, partition, arm_step, profiles, tile_ids, tile_count):
    height = fields.shape[1]
    columns = fields.shape[2] * fields.shape[3]
    padded = extended(fields, (("xy", 2),), 1)
    side_pad = jnp.pad(fields, ((0, 0), (0, 0), (0, 0), (1, 1)))
    laplace = (
        padded[:, :, 2:]
        + padded[:, :, :-2]
        + side_pad[:, :, :, 2:]
        + side_pad[:, :, :, :-2]
        - 4.0 * fields
    )
    source = (fields + lateral[:, None, None, None] * laplace).reshape(4, height, columns)
    face_flow = conductance.reshape(4, height, columns)
    on_top = lax.axis_index("gz") == lax.axis_size("gz") - 1
    keep_mask = jnp.where((jnp.arange(height) == height - 1) & on_top, 0.0, 1.0)
    upper_g = face_flow * keep_mask[None, :, None]
    below_plane = from_behind(face_flow[:, height - 1], "gz", 1)
    lower_g = jnp.concatenate([below_plane[:, None], face_flow[:, : height - 1]], axis=1)
    first_row, last_row, interior = eliminate(-lower_g, 1.0 + lower_g + upper_g, -upper_g, source)
    first_value, last_value = reduced_solve(first_row, last_row, shift_rows, lax.axis_size("gz"))
    solved = assemble(first_value, last_value, interior)
    solved = solved.reshape(fields.shape)
    tile_size = profiles.shape[-1]
    slot_count = profiles.shape[1]
    flat_cells = fields.reshape(4, -1, tile_size)
    tile_rows = tile_ids[0]
    live_count = tile_count[0]
    picked = flat_cells[:, tile_rows]
    slot_pos = jnp.arange(slot_count)
    evolved, change = lever_update(picked, profiles, partition, arm_step)
    live_slot = slot_pos < live_count
    new_profiles = jnp.where(live_slot[None, :, None, None], evolved, 0.0)
    change = jnp.where(live_slot[None, :, None], change, 0.0)
    delta_tiles = (
        jnp.zeros((3, flat_cells.shape[1], tile_size), jnp.float32).at[:, tile_rows].add(change)
    )
    new_fields = jnp.concatenate(
        [solved[:3] + delta_tiles.reshape((3,) + fields.shape[1:]), solved[3:]], axis=0
    )
    return (new_fields, new_profiles)


def solution(mesh):
    return jax.shard_map(
        body,
        mesh=mesh,
        in_specs=(
            P(None, "gz", "xy", None),
            P(None, "gz", "xy", None),
            P(),
            P(),
            P(),
            P(None, ("gz", "xy"), None, None),
            P(("gz", "xy"), None),
            P(("gz", "xy")),
        ),
        out_specs=(P(None, "gz", "xy", None), P(None, ("gz", "xy"), None, None)),
        check_vma=False,
    )
```

profile of v0, /device:TPU:1, one launch (start us, length us, event | category | flops | bytes accessed | tf_op | source)
XLA Modules:
  0.0 406.3 jit_solution(4712287505219111122)
XLA Ops:
  1.8 4.0 collective-permute-start.1
  5.8 1.3 collective-permute-start
  7.7 4.4 %collective-permute-start.2 = (f32[4,8192]{1,0:T(4,128)S(1)}, f32[4,8192]{1,0:T(4,128)S(1)}, u32[]{:S(2)}, u32[]{:S(2)}) collective-permute-start(f32[4,8192]{1,0:T(4,128)S(1)} %bitcast.653), channel_id=1, source_target_pairs={{0,16},{16,32},{32,48},{48,64},{64,80},{80,96},{96,112},{112,128},... | collective-permute-start | bytes 393224 | tf_op jit(solution)/shard_map/ppermute | solution.py:12
  14.6 1.9 fusion.87
  17.7 4.9 %collective-permute-start.4 = (f32[3,4,8192]{2,0,1:T(4,128)S(1)}, f32[3,4,8192]{2,0,1:T(4,128)S(1)}, u32[]{:S(2)}, u32[]{:S(2)}) collective-permute-start(f32[3,4,8192]{2,0,1:T(4,128)S(1)} %pad_maximum_fusion.4), channel_id=1, source_target_pairs={{16,0},{32,16},{48,32},{64,48},{80,64},{96,80},{112,96},{128,112},... | collective-permute-start | bytes 1179656 | tf_op jit(solution)/shard_map/ppermute | solution.py:12
  22.6 6.3 %collective-permute-done.4 = f32[3,4,8192]{2,0,1:T(4,128)S(1)} collective-permute-done((f32[3,4,8192]{2,0,1:T(4,128)S(1)}, f32[3,4,8192]{2,0,1:T(4,128)S(1)}, u32[]{:S(2)}, u32[]{:S(2)}) %collective-permute-start.4) | collective-permute-done | bytes 393248 | tf_op jit(solution)/shard_map/ppermute | solution.py:12
  30.3 1.9 collective-permute-start.3
  32.2 6.1 %collective-permute-done.3 = f32[3,4,8192]{2,0,1:T(4,128)S(1)} collective-permute-done((f32[3,4,8192]{2,0,1:T(4,128)S(1)}, f32[3,4,8192]{2,0,1:T(4,128)S(1)}, u32[]{:S(2)}, u32[]{:S(2)}) %collective-permute-start.3) | collective-permute-done | bytes 393248 | tf_op jit(solution)/shard_map/ppermute | solution.py:12
  40.9 1.9 collective-permute-start.6
  42.8 4.4 %collective-permute-start.5 = (f32[6,4,8192]{2,0,1:T(8,128)S(1)}, f32[6,4,8192]{2,0,1:T(8,128)S(1)}, u32[]{:S(2)}, u32[]{:S(2)}) collective-permute-start(f32[6,4,8192]{2,0,1:T(8,128)S(1)} %concatenate.39), channel_id=1, source_target_pairs={{0,16},{16,32},{32,48},{48,64},{64,80},{80,96},{96,112},{112,128},... | collective-permute-start | bytes 2359304 | tf_op jit(solution)/shard_map/ppermute | solution.py:12
  47.2 10.5 %collective-permute-done.6 = f32[6,4,8192]{2,0,1:T(8,128)S(1)} collective-permute-done((f32[6,4,8192]{2,0,1:T(8,128)S(1)}, f32[6,4,8192]{2,0,1:T(8,128)S(1)}, u32[]{:S(2)}, u32[]{:S(2)}) %collective-permute-start.6) | collective-permute-done | bytes 786464 | tf_op jit(solution)/shard_map/ppermute | solution.py:12
  62.3 1.3 collective-permute-start.8
  63.6 4.4 %collective-permute-start.7 = (f32[6,4,8192]{2,0,1:T(8,128)S(1)}, f32[6,4,8192]{2,0,1:T(8,128)S(1)}, u32[]{:S(2)}, u32[]{:S(2)}) collective-permute-start(f32[6,4,8192]{2,0,1:T(8,128)S(1)} %concatenate.40), channel_id=1, source_target_pairs={{0,32},{16,48},{32,64},{48,80},{64,96},{80,112},{96,128},{112,144}... | collective-permute-start | bytes 2359304 | tf_op jit(solution)/shard_map/ppermute | solution.py:12
  68.0 20.4 %collective-permute-done.8 = f32[6,4,8192]{2,0,1:T(8,128)S(1)} collective-permute-done((f32[6,4,8192]{2,0,1:T(8,128)S(1)}, f32[6,4,8192]{2,0,1:T(8,128)S(1)}, u32[]{:S(2)}, u32[]{:S(2)}) %collective-permute-start.8) | collective-permute-done | bytes 786464 | tf_op jit(solution)/shard_map/ppermute | solution.py:12
  91.3 2.3 concatenate.41
  93.6 1.3 collective-permute-start.10
  94.9 8.6 %collective-permute-start.9 = (f32[6,4,8192]{2,0,1:T(8,128)}, f32[6,4,8192]{2,0,1:T(8,128)S(1)}, u32[]{:S(2)}, u32[]{:S(2)}) collective-permute-start(f32[6,4,8192]{2,0,1:T(8,128)} %concatenate.41), channel_id=1, source_target_pairs={{0,64},{16,80},{32,96},{48,112},{64,128},{80,144},{96,160},{112,17... | collective-permute-start | bytes 2359304 | tf_op jit(solution)/shard_map/ppermute | solution.py:12
  103.5 43.7 %collective-permute-done.10 = f32[6,4,8192]{2,0,1:T(8,128)S(1)} collective-permute-done((f32[6,4,8192]{2,0,1:T(8,128)}, f32[6,4,8192]{2,0,1:T(8,128)S(1)}, u32[]{:S(2)}, u32[]{:S(2)}) %collective-permute-start.10) | collective-permute-done | bytes 786464 | tf_op jit(solution)/shard_map/ppermute | solution.py:12
  149.4 2.3 concatenate.42
  151.7 1.4 collective-permute-start.12
  153.1 12.1 %collective-permute-start.11 = (f32[6,4,8192]{2,0,1:T(8,128)}, f32[6,4,8192]{2,0,1:T(8,128)S(1)}, u32[]{:S(2)}, u32[]{:S(2)}) collective-permute-start(f32[6,4,8192]{2,0,1:T(8,128)} %concatenate.42), channel_id=1, source_target_pairs={{0,128},{16,144},{32,160},{48,176},{64,192},{80,208},{96,224},{112... | collective-permute-start | bytes 2359304 | tf_op jit(solution)/shard_map/ppermute | solution.py:12
  166.1 1.4 copy.24
  168.1 84.9 %collective-permute-done.12 = f32[6,4,8192]{2,0,1:T(8,128)S(1)} collective-permute-done((f32[6,4,8192]{2,0,1:T(8,128)}, f32[6,4,8192]{2,0,1:T(8,128)S(1)}, u32[]{:S(2)}, u32[]{:S(2)}) %collective-permute-start.12) | collective-permute-done | bytes 786464 | tf_op jit(solution)/shard_map/ppermute | solution.py:12
  253.1 1.8 subtract_divide_fusion
  255.0 2.7 multiply_divide_fusion.1
  257.7 3.5 concatenate.43
  261.2 1.3 collective-permute-start.14
  262.5 40.9 %collective-permute-start.13 = (f32[6,4,8192]{2,0,1:T(8,128)}, f32[6,4,8192]{2,0,1:T(8,128)}, u32[]{:S(2)}, u32[]{:S(2)}) collective-permute-start(f32[6,4,8192]{2,0,1:T(8,128)} %concatenate.43), channel_id=1, source_target_pairs={{0,256},{16,272},{32,288},{48,304},{64,320},{80,336},{96,352},{112... | collective-permute-start | bytes 2359304 | tf_op jit(solution)/shard_map/ppermute | solution.py:12
  303.5 34.8 %while.16 = (s32[]{:T(128)}, f32[3,16,64,128]{3,2,1,0:T(8,128)S(1)}, f32[3,64,64]{2,1,0:T(8,128)S(1)}, f32[3]{0:T(128)S(1)}, f32[3,16,128]{2,1,0:T(8,128)S(1)}, ...) while((s32[]{:T(128)}, ...), condition=%wide.region_2.3_spmd, body=%wide.region_0.2_spmd.sunk | while | flops 302413824 | bytes 8175793 | solution.py:43
  303.8 1.5 fusion.129
  306.0 1.5 fusion.129
  308.2 1.5 fusion.129
  310.3 1.5 fusion.129
  312.5 1.5 fusion.129
  314.7 1.5 fusion.129
  316.9 1.5 fusion.129
  319.1 1.5 fusion.129
  321.2 1.5 fusion.129
  323.4 1.5 fusion.129
  325.6 1.5 fusion.129
  327.8 1.5 fusion.129
  330.0 1.5 fusion.129
  332.1 1.5 fusion.129
  334.3 1.5 fusion.129
  336.5 1.5 fusion.129
  339.0 1.4 broadcast_select_fusion
  341.9 32.1 %collective-permute-done.14 = f32[6,4,8192]{2,0,1:T(8,128)} collective-permute-done((f32[6,4,8192]{2,0,1:T(8,128)}, f32[6,4,8192]{2,0,1:T(8,128)}, u32[]{:S(2)}, u32[]{:S(2)}) %collective-permute-start.14) | collective-permute-done | bytes 786464 | tf_op jit(solution)/shard_map/ppermute | solution.py:12
  374.0 30.0 %multiply_subtract_fusion.2 = (f32[4,1,8192]{2,1,0:T(1,128)S(1)}, f32[4,1,8192]{2,1,0:T(1,128)S(1)}, f32[4,1,8192]{2,1,0:T(1,128)S(1)}, f32[4,1,8192]{2,1,0:T(1,...) fusion(f32[4,1,8192]{2,1,0:T(1,128)S(1)} %copy-done.22, f32[4,1,8192]{2,1,0:T(1,128)S(1)} %copy-done.29, ...), kind=kLoop, calls=%fused_computation.213 | loop fusion | flops 6684672 | bytes 10878976 | tf_op jit(solution)/shard_map/sub | solution.py:124
  (238 shorter events, 32.9 us)
Async XLA Ops:
  0.6 6.5 %copy-start.31 = (f32[4,4,8,1024]{3,2,1,0:T(8,128)S(1)}, f32[4,4,8,1024]{3,2,1,0:T(8,128)}, u32[]{:S(2)}) copy-start(f32[4,4,8,1024]{3,2,1,0:T(8,128)} %param.13) | copy-start | bytes 1572868
  1.7 10.5 %copy-start.34 = (f32[4]{0:T(128)S(1)}, f32[4]{0:T(128)}, u32[]{:S(2)}) copy-start(f32[4]{0:T(128)} %param.14) | copy-start | bytes 52
  1.8 10.4 %collective-permute-start.1 = (f32[4,4,1,1024]{3,2,1,0:T(1,128)S(1)}, f32[4,4,1,1024]{3,2,1,0:T(1,128)S(1)}, u32[]{:S(2)}, u32[]{:S(2)}) collective-permute-start(f32[4,4,1,1024]{3,2,1,0:T(1,128)S(1)} %get-tuple-element.283), channel_id=1, source_target_pairs={{0,1},{1,2},{2,3},{3,4},{4,5},{5,6},{6,7},{7,8},{8,9},{9,10},{10,1... | collective-permute-start | bytes 196616 | tf_op jit(solution)/shard_map/ppermute | solution.py:23
  5.8 6.3 %collective-permute-start = (f32[4,4,1,1024]{3,2,1,0:T(1,128)S(1)}, f32[4,4,1,1024]{3,2,1,0:T(1,128)S(1)}, u32[]{:S(2)}, u32[]{:S(2)}) collective-permute-start(f32[4,4,1,1024]{3,2,1,0:T(1,128)S(1)} %get-tuple-element.282), channel_id=1, source_target_pairs={{1,0},{2,1},{3,2},{4,3},{5,4},{6,5},{7,6},{8,7},{9,8},{10,9},{11,1... | collective-permute-start | bytes 196616 | tf_op jit(solution)/shard_map/ppermute | solution.py:25
  7.7 6.3 %collective-permute-start.2 = (f32[4,8192]{1,0:T(4,128)S(1)}, f32[4,8192]{1,0:T(4,128)S(1)}, u32[]{:S(2)}, u32[]{:S(2)}) collective-permute-start(f32[4,8192]{1,0:T(4,128)S(1)} %bitcast.653), channel_id=1, source_target_pairs={{0,16},{16,32},{32,48},{48,64},{64,80},{80,96},{96,112},{112,128},... | collective-permute-start | bytes 393224 | tf_op jit(solution)/shard_map/ppermute | solution.py:12
  13.0 16.0 %copy-start.7 = (f32[4,4,8192]{2,1,0:T(4,128)}, f32[4,4,8192]{2,1,0:T(4,128)S(1)}, u32[]{:S(2)}) copy-start(f32[4,4,8192]{2,1,0:T(4,128)S(1)} %reshape.1592) | copy-start | bytes 1572868
  14.6 2.4 copy-start.5
  14.6 14.4 %copy-start.1 = (f32[4,4,8192]{2,1,0:T(4,128)}, f32[4,4,8192]{2,1,0:T(4,128)S(1)}, u32[]{:S(2)}) copy-start(f32[4,4,8192]{2,1,0:T(4,128)S(1)} %get-tuple-element.279) | copy-start | bytes 1572868
  14.6 14.3 %copy-start.3 = (f32[4,4,8192]{2,1,0:T(4,128)}, f32[4,4,8192]{2,1,0:T(4,128)S(1)}, u32[]{:S(2)}) copy-start(f32[4,4,8192]{2,1,0:T(4,128)S(1)} %get-tuple-element.278) | copy-start | bytes 1572868
  16.6 13.4 %copy-start.21 = (f32[4,1,8192]{2,1,0:T(1,128)}, f32[4,1,8192]{2,1,0:T(1,128)S(1)}, u32[]{:S(2)}) copy-start(f32[4,1,8192]{2,1,0:T(1,128)S(1)} %get-tuple-element.246) | copy-start | bytes 393220
  17.7 11.2 %collective-permute-start.4 = (f32[3,4,8192]{2,0,1:T(4,128)S(1)}, f32[3,4,8192]{2,0,1:T(4,128)S(1)}, u32[]{:S(2)}, u32[]{:S(2)}) collective-permute-start(f32[3,4,8192]{2,0,1:T(4,128)S(1)} %pad_maximum_fusion.4), channel_id=1, source_target_pairs={{16,0},{32,16},{48,32},{64,48},{80,64},{96,80},{112,96},{128,112},... | collective-permute-start | bytes 1179656 | tf_op jit(solution)/shard_map/ppermute | solution.py:12
  29.0 10.1 %copy-start.27 = (f32[3,4,8192]{2,0,1:T(4,128)}, f32[3,4,8192]{2,0,1:T(4,128)S(1)}, u32[]{:S(2)}) copy-start(f32[3,4,8192]{2,0,1:T(4,128)S(1)} %collective-permute-done.4) | copy-start | bytes 1179652
  30.3 8.0 %collective-permute-start.3 = (f32[3,4,8192]{2,0,1:T(4,128)S(1)}, f32[3,4,8192]{2,0,1:T(4,128)S(1)}, u32[]{:S(2)}, u32[]{:S(2)}) collective-permute-start(f32[3,4,8192]{2,0,1:T(4,128)S(1)} %pad_maximum_fusion.3), channel_id=1, source_target_pairs={{0,16},{16,32},{32,48},{48,64},{64,80},{80,96},{96,112},{112,128},... | collective-permute-start | bytes 1179656 | tf_op jit(solution)/shard_map/ppermute | solution.py:12
  40.9 16.9 %collective-permute-start.6 = (f32[6,4,8192]{2,0,1:T(8,128)S(1)}, f32[6,4,8192]{2,0,1:T(8,128)S(1)}, u32[]{:S(2)}, u32[]{:S(2)}) collective-permute-start(f32[6,4,8192]{2,0,1:T(8,128)S(1)} %concatenate.39), channel_id=1, source_target_pairs={{16,0},{32,16},{48,32},{64,48},{80,64},{96,80},{112,96},{128,112},... | collective-permute-start | bytes 2359304 | tf_op jit(solution)/shard_map/ppermute | solution.py:12
  42.8 16.1 %collective-permute-start.5 = (f32[6,4,8192]{2,0,1:T(8,128)S(1)}, f32[6,4,8192]{2,0,1:T(8,128)S(1)}, u32[]{:S(2)}, u32[]{:S(2)}) collective-permute-start(f32[6,4,8192]{2,0,1:T(8,128)S(1)} %concatenate.39), channel_id=1, source_target_pairs={{0,16},{16,32},{32,48},{48,64},{64,80},{80,96},{96,112},{112,128},... | collective-permute-start | bytes 2359304 | tf_op jit(solution)/shard_map/ppermute | solution.py:12
  57.8 3.2 copy-start.11
  58.9 2.1 copy-start.12
  62.3 26.1 %collective-permute-start.8 = (f32[6,4,8192]{2,0,1:T(8,128)S(1)}, f32[6,4,8192]{2,0,1:T(8,128)S(1)}, u32[]{:S(2)}, u32[]{:S(2)}) collective-permute-start(f32[6,4,8192]{2,0,1:T(8,128)S(1)} %concatenate.40), channel_id=1, source_target_pairs={{32,0},{48,16},{64,32},{80,48},{96,64},{112,80},{128,96},{144,112}... | collective-permute-start | bytes 2359304 | tf_op jit(solution)/shard_map/ppermute | solution.py:12
  63.6 25.7 %collective-permute-start.7 = (f32[6,4,8192]{2,0,1:T(8,128)S(1)}, f32[6,4,8192]{2,0,1:T(8,128)S(1)}, u32[]{:S(2)}, u32[]{:S(2)}) collective-permute-start(f32[6,4,8192]{2,0,1:T(8,128)S(1)} %concatenate.40), channel_id=1, source_target_pairs={{0,32},{16,48},{32,64},{48,80},{64,96},{80,112},{96,128},{112,144}... | collective-permute-start | bytes 2359304 | tf_op jit(solution)/shard_map/ppermute | solution.py:12
  88.4 2.9 copy-start.13
  89.2 2.1 copy-start.14
  93.6 53.6 %collective-permute-start.10 = (f32[6,4,8192]{2,0,1:T(8,128)}, f32[6,4,8192]{2,0,1:T(8,128)S(1)}, u32[]{:S(2)}, u32[]{:S(2)}) collective-permute-start(f32[6,4,8192]{2,0,1:T(8,128)} %concatenate.41), channel_id=1, source_target_pairs={{64,0},{80,16},{96,32},{112,48},{128,64},{144,80},{160,96},{176,11... | collective-permute-start | bytes 2359304 | tf_op jit(solution)/shard_map/ppermute | solution.py:12
  94.9 52.3 %collective-permute-start.9 = (f32[6,4,8192]{2,0,1:T(8,128)}, f32[6,4,8192]{2,0,1:T(8,128)S(1)}, u32[]{:S(2)}, u32[]{:S(2)}) collective-permute-start(f32[6,4,8192]{2,0,1:T(8,128)} %concatenate.41), channel_id=1, source_target_pairs={{0,64},{16,80},{32,96},{48,112},{64,128},{80,144},{96,160},{112,17... | collective-permute-start | bytes 2359304 | tf_op jit(solution)/shard_map/ppermute | solution.py:12
  147.2 2.1 copy-start.15
  147.2 2.1 copy-start.16
  149.3 103.8 %copy-start.19 = (f32[1,4,8192]{2,0,1:T(1,128)}, f32[1,4,8192]{2,0,1:T(1,128)S(1)}, u32[]{:S(2)}) copy-start(f32[1,4,8192]{2,0,1:T(1,128)S(1)} %get-tuple-element.288) | copy-start | bytes 393220
  149.3 103.7 %copy-start.20 = (f32[1,4,8192]{2,0,1:T(1,128)}, f32[1,4,8192]{2,0,1:T(1,128)S(1)}, u32[]{:S(2)}) copy-start(f32[1,4,8192]{2,0,1:T(1,128)S(1)} %get-tuple-element.289) | copy-start | bytes 393220
  149.4 18.1 %copy-start.36 = (s32[1,16]{1,0:T(1,128)S(1)}, s32[1,16]{1,0:T(1,128)}, u32[]{:S(2)}) copy-start(s32[1,16]{1,0:T(1,128)} %param.18) | copy-start | bytes 196
  151.6 101.4 %copy-start.24 = (f32[1,4,8192]{2,0,1:T(1,128)S(1)}, f32[1,4,8192]{2,0,1:T(1,128)}, u32[]{:S(2)}) copy-start(f32[1,4,8192]{2,0,1:T(1,128)} %copy-done.23) | copy-start | bytes 393220
  151.6 101.5 %copy-start.26 = (f32[1,4,8192]{2,0,1:T(1,128)S(1)}, f32[1,4,8192]{2,0,1:T(1,128)}, u32[]{:S(2)}) copy-start(f32[1,4,8192]{2,0,1:T(1,128)} %copy-done.25) | copy-start | bytes 393220
  151.7 101.4 %collective-permute-start.12 = (f32[6,4,8192]{2,0,1:T(8,128)}, f32[6,4,8192]{2,0,1:T(8,128)S(1)}, u32[]{:S(2)}, u32[]{:S(2)}) collective-permute-start(f32[6,4,8192]{2,0,1:T(8,128)} %concatenate.42), channel_id=1, source_target_pairs={{128,0},{144,16},{160,32},{176,48},{192,64},{208,80},{224,96},{240... | collective-permute-start | bytes 2359304 | tf_op jit(solution)/shard_map/ppermute | solution.py:12
  153.1 100.0 %collective-permute-start.11 = (f32[6,4,8192]{2,0,1:T(8,128)}, f32[6,4,8192]{2,0,1:T(8,128)S(1)}, u32[]{:S(2)}, u32[]{:S(2)}) collective-permute-start(f32[6,4,8192]{2,0,1:T(8,128)} %concatenate.42), channel_id=1, source_target_pairs={{0,128},{16,144},{32,160},{48,176},{64,192},{80,208},{96,224},{112... | collective-permute-start | bytes 2359304 | tf_op jit(solution)/shard_map/ppermute | solution.py:12
  168.1 86.9 %copy-start.32 = (f32[16,4,128]{2,1,0:T(4,128)}, f32[16,4,128]{2,1,0:T(4,128)S(1)}, u32[]{:S(2)}) copy-start(f32[16,4,128]{2,1,0:T(4,128)S(1)} %gather_fusion) | copy-start | bytes 98308
  253.1 4.6 %copy-start.17 = (f32[6,4,8192]{2,0,1:T(8,128)}, f32[6,4,8192]{2,0,1:T(8,128)S(1)}, u32[]{:S(2)}) copy-start(f32[6,4,8192]{2,0,1:T(8,128)S(1)} %collective-permute-done.12) | copy-start | bytes 2359300
  253.1 1.9 copy-start.18
  255.0 48.5 %copy-start = (f32[3,16,64,128]{3,2,1,0:T(8,128)S(1)}, f32[3,16,64,128]{3,2,1,0:T(8,128)}, u32[]{:S(2)}) copy-start(f32[3,16,64,128]{3,2,1,0:T(8,128)} %param.17) | copy-start | bytes 4718596
  255.0 48.5 %copy-start.10 = (f32[3,64,64]{2,1,0:T(8,128)S(1)}, f32[3,64,64]{2,1,0:T(8,128)}, u32[]{:S(2)}) copy-start(f32[3,64,64]{2,1,0:T(8,128)} %param.16) | copy-start | bytes 147460
  255.0 48.5 %copy-start.35 = (f32[3]{0:T(128)S(1)}, f32[3]{0:T(128)}, u32[]{:S(2)}) copy-start(f32[3]{0:T(128)} %param.15) | copy-start | bytes 40
  261.2 112.7 %collective-permute-start.14 = (f32[6,4,8192]{2,0,1:T(8,128)}, f32[6,4,8192]{2,0,1:T(8,128)}, u32[]{:S(2)}, u32[]{:S(2)}) collective-permute-start(f32[6,4,8192]{2,0,1:T(8,128)} %concatenate.43), channel_id=1, source_target_pairs={{256,0},{272,16},{288,32},{304,48},{320,64},{336,80},{352,96},{368... | collective-permute-start | bytes 2359304 | tf_op jit(solution)/shard_map/ppermute | solution.py:12
  262.5 111.4 %collective-permute-start.13 = (f32[6,4,8192]{2,0,1:T(8,128)}, f32[6,4,8192]{2,0,1:T(8,128)}, u32[]{:S(2)}, u32[]{:S(2)}) collective-permute-start(f32[6,4,8192]{2,0,1:T(8,128)} %concatenate.43), channel_id=1, source_target_pairs={{0,256},{16,272},{32,288},{48,304},{64,320},{80,336},{96,352},{112... | collective-permute-start | bytes 2359304 | tf_op jit(solution)/shard_map/ppermute | solution.py:12
  339.0 1.5 copy-start.33
  339.0 34.9 %copy-start.30 = (f32[4,1,8192]{2,1,0:T(1,128)S(1)}, f32[4,1,8192]{2,1,0:T(1,128)}, u32[]{:S(2)}) copy-start(f32[4,1,8192]{2,1,0:T(1,128)} %get-tuple-element.244) | copy-start | bytes 393220
  340.4 33.5 %copy-start.2 = (f32[4,4,8192]{2,1,0:T(4,128)S(1)}, f32[4,4,8192]{2,1,0:T(4,128)}, u32[]{:S(2)}) copy-start(f32[4,4,8192]{2,1,0:T(4,128)} %copy-done.1) | copy-start | bytes 1572868
  340.4 33.5 %copy-start.4 = (f32[4,4,8192]{2,1,0:T(4,128)S(1)}, f32[4,4,8192]{2,1,0:T(4,128)}, u32[]{:S(2)}) copy-start(f32[4,4,8192]{2,1,0:T(4,128)} %copy-done.3) | copy-start | bytes 1572868
  340.4 33.5 %copy-start.6 = (f32[4,4,8192]{2,1,0:T(4,128)S(1)}, f32[4,4,8192]{2,1,0:T(4,128)}, u32[]{:S(2)}) copy-start(f32[4,4,8192]{2,1,0:T(4,128)} %copy-done.5) | copy-start | bytes 1572868
  340.4 33.5 %copy-start.8 = (f32[4,4,8192]{2,1,0:T(4,128)S(1)}, f32[4,4,8192]{2,1,0:T(4,128)}, u32[]{:S(2)}) copy-start(f32[4,4,8192]{2,1,0:T(4,128)} %copy-done.7) | copy-start | bytes 1572868
  340.4 33.5 %copy-start.22 = (f32[4,1,8192]{2,1,0:T(1,128)S(1)}, f32[4,1,8192]{2,1,0:T(1,128)}, u32[]{:S(2)}) copy-start(f32[4,1,8192]{2,1,0:T(1,128)} %copy-done.21) | copy-start | bytes 393220
  340.5 33.5 %copy-start.29 = (f32[4,1,8192]{2,1,0:T(1,128)S(1)}, f32[4,1,8192]{2,1,0:T(1,128)}, u32[]{:S(2)}) copy-start(f32[4,1,8192]{2,1,0:T(1,128)} %get-tuple-element.241) | copy-start | bytes 393220
  (4 other events, 4.2 us)
where the time goes:
time: 409 us; the launch traced here: 406 us
  waiting for transfers between devices  207 us (51%)
  starting transfers between devices  94.1 us (23%)
  other arithmetic  56 us (14%)
  matrix products  24.6 us (6%)
  local copies, waits for them, and re-layouts  21.2 us (5%)
    ppermute x13, waiting for transfers between devices, from_behind(): return lax.ppermute(block, axis, route)  207 us
    ppermute x13, starting transfers between devices, from_behind(): return lax.ppermute(block, axis, route)  88.8 us
    sub x2, other arithmetic, assemble(): back_rhs[row_at] - back_first[row_at] * first_value  30.4 us
    dot_general x16, matrix products, substep(): jnp.einsum('jab,jsbc->jsac', arm_step, current, precision=lax.Precision.H...  24.6 us
    concatenate x5, local copies, waits for them, and re-layouts, reduced_solve(): paired_rows = jnp.concatenate([first_row, last_row], axis=0)  10.5 us
  transfers between devices with their start and end apart: 15, of which 10 were waited for; matrix products, arithmetic and copies ran while one was open for 10% of the time, Pallas kernels for 0%

commit v1 on v0

v1 whole, which is shorter than its diff:
```python
import functools

import jax
import jax.numpy as jnp
from jax import lax
from jax.experimental import pallas as pl
from jax.experimental.pallas import tpu as pltpu
from jax.sharding import PartitionSpec as P

F32 = jnp.float32
BF16 = jnp.bfloat16
MESH = pl.DeviceIdType.MESH
HIGH = lax.Precision.HIGHEST
SUB = 16
ARM = 64
SLOTS = 16
DELTAS = (3, -3, 2, -2, 1, -1)

ORDER = {}
BASE = {}
for _delta in (0,) + DELTAS:
    BASE[_delta] = len(ORDER)
    for _i in range(max(0, -_delta), min(4, 4 - _delta)):
        ORDER[(_i, _i + _delta)] = len(ORDER)
COUNT = {d: 4 - abs(d) for d in DELTAS}


def merge_mass(low, high):
    mass = low[2] + high[1]
    inverse = 1.0 / (mass + low[0] + high[0])
    a, b = low[0] * inverse, high[0] * inverse
    return (a * high[0], low[1] + a * mass, high[2] + b * mass), (a, b, inverse)


def merge_rhs(low, high, a, b, inverse):
    rhs = low[1] + high[0]
    return (low[0] + a * rhs, high[1] + b * rhs), rhs * inverse


def split(x):
    high = x.astype(BF16).astype(F32)
    return high, x - high


def dot(x, y, precision=None):
    return jnp.dot(x, y, precision=precision, preferred_element_type=F32)


def kernel(
    n_xy,
    fields, cond, lateral, partition, arm, profiles, ids, ids_row, count,
    out_fields, out_profiles,
    fld, cnd, src, prof, coef, tail,
    halo_s, halo_r,
    pair_cs, pair_rs, blk_c, blk_r, chip_coef,
    l1_cs, l1_rs, l1_cr, l1_rr, sup_coef,
    l2_cs, l2_rs, l2_cr, l2_rr, ret_s, ret_r,
    back_s, back_r, fin, fin_r,
    cells, wsc, gsc, hsc, lhs1, lhs2, ysc, ssc, change, delta,
    in_sem, prof_sem, out_sem, pout_sem,
    send_sem, recv_sem,
):
    gz = lax.axis_index("gz")
    xy = lax.axis_index("xy")
    core = lax.rem(gz, 2)
    chip = gz // 2
    other = 1 - core
    ring = chip // 4
    phase = lax.rem(chip, 4)

    def at_chip(offset):
        return (lax.rem(chip + (offset + 16), 16) * 2 + core, xy)

    left = (gz, lax.rem(xy + n_xy - 1, n_xy))
    right = (gz, lax.rem(xy + 1, n_xy))
    peer = (chip * 2 + other, xy)

    def load(ref, buf, base, y, sem):
        return pltpu.make_async_copy(
            ref.at[:, pl.ds(128 * y, 128)], buf.at[y + base], in_sem.at[sem + y]
        )

    field_loads = [load(fields, fld, 1, y, 0) for y in range(8)]
    cond_loads = [load(cond, cnd, 0, y, 8) for y in range(8)]
    prof_loads = [
        pltpu.make_async_copy(
            profiles.at[pl.ds(1024 * j, 1024)], prof.at[pl.ds(1024 * j, 1024)], prof_sem.at[j]
        )
        for j in range(3)
    ]
    barrier = pltpu.get_barrier_semaphore()
    partners = [left, right, peer]
    partners += [at_chip(d) for d in DELTAS] + [at_chip(4 * d) for d in (1, 2, 3)]
    for partner in partners:
        pl.semaphore_signal(barrier, inc=1, device_id=partner, device_id_type=MESH)
    for copy in field_loads + cond_loads + prof_loads:
        copy.start()

    sends = []
    used = [0]

    def remote(source, target, device):
        n = used[0]
        used[0] = n + 1
        copy = pltpu.make_async_remote_copy(
            src_ref=source, dst_ref=target, send_sem=send_sem.at[n], recv_sem=recv_sem.at[n],
            device_id=device, device_id_type=MESH,
        )
        copy.start()
        sends.append(copy)
        return copy

    fld[0] = jnp.zeros((128, 128), F32)
    fld[9] = jnp.zeros((128, 128), F32)
    for copy in field_loads:
        copy.wait()
    for y in range(8):
        halo_s[0, y] = fld[y + 1, pl.ds(0, 16, stride=8), :]
        halo_s[1, y] = fld[y + 1, pl.ds(7, 16, stride=8), :]
    pl.semaphore_wait(barrier, len(partners))
    halo = [
        remote(halo_s.at[0], halo_r.at[1], left),
        remote(halo_s.at[1], halo_r.at[0], right),
    ]

    keep = jnp.where(gz == lax.axis_size("gz") - 1, 0.0, 1.0).astype(F32)
    for copy in cond_loads:
        copy.wait()

    def plane(buf, y, f, z):
        return buf[y, pl.ds(pl.multiple_of(f * 32 + z * 8, 8), 8), :]

    def eliminate_mass(owner, p):
        f, y = owner * 2 + p // 8, lax.rem(p, 8)
        e = owner * 16 + p
        block = (plane(cnd, y, f, 0), 1.0, 0.0)
        for z in (1, 2, 3):
            face = plane(cnd, y, f, z)
            if z == 3:
                face = face * keep
            block, held = merge_mass(block, (face, 1.0, 0.0))
            for n in range(3):
                coef[e, 3 * z - 3 + n] = held[n]
        return block

    @pl.loop(0, 16, unroll=4)
    def _(p):
        block = eliminate_mass(other, p)
        for n in range(3):
            pair_cs[p, n] = block[n]

    pair_c = remote(pair_cs, blk_c.at[core], peer)

    @pl.loop(0, 16, unroll=4)
    def _(p):
        block = eliminate_mass(core, p)
        for n in range(3):
            blk_c[core, p, n] = block[n]

    row = lax.broadcasted_iota(jnp.int32, (8, 128), 0)
    lane = lax.broadcasted_iota(jnp.int32, (8, 128), 1)

    @pl.loop(0, 16)
    def _(q):
        at = pl.ds(pl.multiple_of(q * 8, 8), 8)
        rate = lateral[q // 4]
        tiles = [fld[y, at, :] for y in range(10)]
        for y in range(8):
            before, here, after = tiles[y : y + 3]
            down = jnp.where(row == 0, 0.0, pltpu.roll(here, 1, 0))
            up = jnp.where(row == 7, 0.0, pltpu.roll(here, 7, 0))
            low = pltpu.roll(jnp.where(lane == 127, before, here), 1, 1)
            high = pltpu.roll(jnp.where(lane == 0, after, here), 127, 1)
            src[y, at, :] = here + rate * (down + up + low + high - 4.0 * here)

    def powers(j):
        power = arm[j]
        wsc[j] = jnp.full((32, ARM), 1.0 / ARM, F32)
        last = lax.broadcasted_iota(jnp.int32, (ARM, SUB), 0) == ARM - 1
        gsc[j] = jnp.where(last, 1.0, 0.0).astype(F32)
        n = 1
        while n < SUB:
            both = dot(jnp.concatenate([power, wsc[j, 0:8]], axis=0), power, HIGH)
            tips = dot(power, gsc[j], HIGH)
            wsc[j, n : 2 * n] = both[ARM : ARM + n]
            gsc[j, :, n : 2 * n] = tips[:, 0:n]
            power = both[:ARM]
            n *= 2
        wsc[j, SUB : SUB + 1] = jnp.sum(power, axis=0, keepdims=True) * (1.0 / ARM)
        rows = wsc[j]
        end = lax.broadcasted_iota(jnp.int32, (SUB, ARM), 1) == ARM - 1
        held = jnp.sum(jnp.where(end, rows[:SUB], 0.0), axis=1, keepdims=True)
        hsc[j] = jnp.broadcast_to(held, (SUB, 128))
        for n, part in enumerate(split(rows)):
            lhs1[j, :, 128 * n : 128 * n + 64] = part
            lhs1[j, :, 128 * n + 64 : 128 * n + 128] = part
        high, low = split(power)
        lhs2[j, :, 0:64] = high
        lhs2[j, :, 64:128] = high
        lhs2[j, :, 128:192] = low
        high, low = split(gsc[j])
        lhs2[j, :, 192:208] = high
        lhs2[j, :, 208:224] = high
        lhs2[j, :, 224:240] = low
        lhs2[j, :, 240:256] = low

    for j in range(3):
        powers(j)

    for copy in halo:
        copy.wait_recv()
    first = jnp.where(xy == 0, 0.0, 1.0).astype(F32)
    final = jnp.where(xy == n_xy - 1, 0.0, 1.0).astype(F32)

    def eliminate_rhs(owner, p):
        f, y = owner * 2 + p // 8, lax.rem(p, 8)
        e = owner * 16 + p
        rate = lateral[f]
        block = None
        for z in range(4):
            edge = jnp.where(row == 0, halo_r[0, y, pl.ds(f * 4 + z, 1), :] * (rate * first), 0.0)
            edge += jnp.where(row == 7, halo_r[1, y, pl.ds(f * 4 + z, 1), :] * (rate * final), 0.0)
            here = plane(src, y, f, z) + edge
            if z == 0:
                block = (here, 0.0)
            else:
                block, tail[e, z - 1] = merge_rhs(
                    block, (here, 0.0), *(coef[e, 3 * z - 3 + n] for n in range(3))
                )
        return block

    @pl.loop(0, 16, unroll=4)
    def _(p):
        block = eliminate_rhs(other, p)
        for n in range(2):
            pair_rs[p, n] = block[n]

    pair_r = remote(pair_rs, blk_r.at[core], peer)

    @pl.loop(0, 16, unroll=4)
    def _(p):
        block = eliminate_rhs(core, p)
        for n in range(2):
            blk_r[core, p, n] = block[n]

    def part_of(i, m):
        return lax.rem(phase + 4 - i, 4) * 4 + m

    pair_c.wait_recv()
    for (i, m), s in ORDER.items():
        p = part_of(i, m)
        merged, held = merge_mass(*([blk_c[c, p, n] for n in range(3)] for c in range(2)))
        target = l1_cr if i == m else l1_cs
        for n in range(3):
            chip_coef[s, n] = held[n]
            target[s, n] = merged[n]

    def spread(source, target, sign):
        return [
            remote(
                source.at[pl.ds(BASE[d], COUNT[d])], target.at[pl.ds(BASE[d], COUNT[d])],
                at_chip(sign * d),
            )
            for d in DELTAS
        ]

    l1_c = spread(l1_cs, l1_cr, 1)
    pair_r.wait_recv()
    for (i, m), s in ORDER.items():
        p = part_of(i, m)
        merged, ratio = merge_rhs(
            *([blk_r[c, p, n] for n in range(2)] for c in range(2)),
            *(chip_coef[s, n] for n in range(3)),
        )
        chip_coef[s, 2] = ratio
        target = l1_rr if i == m else l1_rs
        for n in range(2):
            target[s, n] = merged[n]
    l1_r = spread(l1_rs, l1_rr, 1)

    for copy in prof_loads:
        copy.wait()

    def tile_pair(j, t):
        at = [pl.multiple_of(j * 1024 + t * 128 + 64 * n, 64) for n in range(2)]
        return at, jnp.concatenate([prof[pl.ds(a, 64), :] for a in at], axis=1)

    @pl.loop(0, 8)
    def _(t):
        for j in range(3):
            unused, tile = tile_pair(j, t)
            high, low = (part.astype(BF16) for part in split(tile))
            means = dot(lhs1[j].astype(BF16), jnp.concatenate([high, low, high, low], axis=0))
            for n in range(2):
                ysc[j, pl.ds(pl.multiple_of(t * 64 + 32 * n, 32), 32), :] = means[:, 128 * n : 128 * n + 128]

    for slot in range(SLOTS):
        tile = ids[0, slot]
        y, at = lax.rem(tile, 8), (tile // 64) * 8 + lax.rem(tile // 8, 8)
        for f in range(4):
            cells[f, slot : slot + 1] = fld[y + 1, pl.ds(f * 32 + at, 1), :]

    def group(buf, m, n_values):
        return [[buf[ORDER[(i, m)], n] for n in range(n_values)] for i in range(4)]

    def slot_of(m):
        return lax.rem(m + 4 - ring, 4)

    for copy in l1_c:
        copy.wait_recv()
    for m in range(4):
        blocks = group(l1_cr, m, 3)
        low, held1 = merge_mass(blocks[0], blocks[1])
        high, held3 = merge_mass(blocks[2], blocks[3])
        merged, held2 = merge_mass(low, high)
        for k, held in enumerate((held1, held2, held3)):
            for n in range(3):
                sup_coef[m, k, n] = held[n]
        for n in range(3):
            l2_cs[slot_of(m), n] = merged[n]
    l2_c = [remote(l2_cs.at[d], l2_cr.at[4 - d], at_chip(4 * d)) for d in (2, 1, 3)]
    for copy in l1_r:
        copy.wait_recv()
    for m in range(4):
        blocks = group(l1_rr, m, 2)
        held = [[sup_coef[m, k, n] for n in range(3)] for k in range(3)]
        low, ratio1 = merge_rhs(blocks[0], blocks[1], *held[0])
        high, ratio3 = merge_rhs(blocks[2], blocks[3], *held[2])
        merged, ratio2 = merge_rhs(low, high, *held[1])
        for k, ratio in enumerate((ratio1, ratio2, ratio3)):
            sup_coef[m, k, 2] = ratio
        for n in range(2):
            l2_rs[slot_of(m), n] = merged[n]
    l2_r = [remote(l2_rs.at[d], l2_rr.at[4 - d], at_chip(4 * d)) for d in (2, 1, 3)]

    live = lax.broadcasted_iota(jnp.int32, (SLOTS, 128), 0) < count[0]
    solid = 0.9 / (1.0 + jnp.exp(cells[3]))
    inverses = [1.0 / (1.0 - solid * ((k + 1) / SUB)) for k in range(SUB)]
    for j in range(3):
        solute = cells[j]
        half = 0.5 * partition[j]
        liquids = []
        for k in range(SUB + 1):
            mean = ysc[j, pl.ds(k, SLOTS, stride=32), :]
            for i in range(k):
                mean += hsc[j, k - 1 - i : k - i, :] * liquids[i]
            if k == SUB:
                moved = solid * (mean - partition[j] * solute)
                change[:, 128 * j : 128 * j + 128] = jnp.where(live, moved, 0.0)
            else:
                fraction = solid * ((k + 1) / SUB)
                liquids.append(half * ((solute - fraction * mean) * inverses[k]))
                ssc[j, pl.ds(SUB - 1 - k, SLOTS, stride=SUB), :] = liquids[k]

    for copy in l2_c:
        copy.wait_recv()
    masses = [[(l2_cr if b else l2_cs)[b, n] for n in range(3)] for b in range(4)]
    low, held1 = merge_mass(masses[0], masses[1])
    high, held3 = merge_mass(masses[2], masses[3])
    whole, held2 = merge_mass(low, high)
    for copy in l2_r:
        copy.wait_recv()
    rhs = [[(l2_rr if b else l2_rs)[b, n] for n in range(2)] for b in range(4)]
    low, ratio1 = merge_rhs(rhs[0], rhs[1], *held1)
    high, ratio3 = merge_rhs(rhs[2], rhs[3], *held3)
    total, ratio2 = merge_rhs(low, high, *held2)
    v0 = (total[0] + total[1]) / (whole[1] + whole[2])
    v2 = ratio2 + (held2[0] + held2[1]) * v0
    v1 = ratio1 + held1[0] * v0 + held1[1] * v2
    v3 = ratio3 + held3[0] * v2 + held3[1] * v0
    values = [v0, v1, v2, v3, v0]
    for b in range(4):
        target = ret_s if b else ret_r
        target[b, 0] = values[b]
        target[b, 1] = values[b + 1]
    ret = [remote(ret_s.at[b], ret_r.at[4 - b], at_chip(4 * b)) for b in (2, 1, 3)]

    def evolve(j):
        @pl.loop(0, 8)
        def _(t):
            at, tile = tile_pair(j, t)
            tips = jnp.concatenate(
                [ssc[j, pl.ds(pl.multiple_of(t * 32 + 16 * n, 16), 16), :] for n in range(2)], axis=1
            )
            high, low = (part.astype(BF16) for part in split(tile))
            tip_high, tip_low = (part.astype(BF16) for part in split(tips))
            evolved = dot(
                lhs2[j].astype(BF16),
                jnp.concatenate(
                    [high, low, high, tip_high, tip_low, tip_high, tip_low], axis=0
                ),
            )
            for n in range(2):
                shown = jnp.full((ARM, 128), 2 * t + n, jnp.int32) < count[0]
                prof[pl.ds(at[n], 64), :] = jnp.where(
                    shown, evolved[:, 128 * n : 128 * n + 128], 0.0
                )

        copy = pltpu.make_async_copy(
            prof.at[pl.ds(1024 * j, 1024)], out_profiles.at[pl.ds(1024 * j, 1024)], pout_sem.at[j]
        )
        copy.start()
        return copy

    stores = [evolve(0)]

    for copy in ret:
        copy.wait_recv()
    for m in range(4):
        s = slot_of(m)
        x0, x4 = ret_r[s, 0], ret_r[s, 1]
        held = [[sup_coef[m, k, n] for n in range(3)] for k in range(3)]
        x2 = held[1][2] + held[1][0] * x0 + held[1][1] * x4
        x1 = held[0][2] + held[0][0] * x0 + held[0][1] * x2
        x3 = held[2][2] + held[2][0] * x2 + held[2][1] * x4
        values = [x0, x1, x2, x3, x4]
        for i in range(4):
            target = back_r if i == m else back_s
            for n in range(2):
                target[ORDER[(i, m)], n] = values[i + n]
    back = spread(back_s, back_r, -1)

    stores.append(evolve(1))
    stores.append(evolve(2))

    place = lax.broadcasted_iota(jnp.int32, (256, SLOTS), 0)
    named = (place // 64) * 64 + lax.rem(place, 8) * 8 + lax.rem(place // 8, 8)
    hit = jnp.where(named == ids_row[...], 1.0, 0.0).astype(BF16)
    rest = change[...]
    spreads = None
    for n in range(3):
        piece = rest.astype(BF16)
        rest = rest - piece.astype(F32)
        term = dot(hit, piece)
        spreads = term if spreads is None else spreads + term
    for j in range(3):
        delta[j] = spreads[:, 128 * j : 128 * j + 128]
    delta[3] = jnp.zeros((256, 128), F32)

    for copy in back:
        copy.wait_recv()
    for (i, m), s in ORDER.items():
        p = part_of(i, m)
        low, high = back_r[s, 0], back_r[s, 1]
        middle = chip_coef[s, 2] + chip_coef[s, 0] * low + chip_coef[s, 1] * high
        fin[0, p, 0] = low
        fin[0, p, 1] = middle
        fin[1, p, 0] = middle
        fin[1, p, 1] = high
    last = remote(fin.at[other], fin_r, peer)

    def finish(owner, p, low, high):
        f, y = owner * 2 + p // 8, lax.rem(p, 8)
        e = owner * 16 + p
        above = high
        values = [low, None, None, None]
        for z in (3, 2, 1):
            above = tail[e, z - 1] + coef[e, 3 * z - 3] * low + coef[e, 3 * z - 2] * above
            values[z] = above
        for z in range(4):
            at = pl.ds(pl.multiple_of(f * 32 + z * 8, 8), 8)
            src[y, at, :] = values[z] + delta[f, pl.ds(pl.multiple_of(z * 64 + y * 8, 8), 8), :]

    def store(owner, n):
        for y in range(8):
            rows = pl.ds(pl.multiple_of(owner * 64, 64), 64)
            copy = pltpu.make_async_copy(
                src.at[y, rows], out_fields.at[rows, pl.ds(128 * y, 128)], out_sem.at[n + y]
            )
            copy.start()
            stores.append(copy)

    @pl.loop(0, 16, unroll=4)
    def _(p):
        finish(core, p, fin[core, p, 0], fin[core, p, 1])

    store(core, 0)
    last.wait_recv()

    @pl.loop(0, 16, unroll=4)
    def _(p):
        finish(other, p, fin_r[p, 0], fin_r[p, 1])

    store(other, 8)
    for copy in sends:
        copy.wait_send()
    for copy in stores:
        copy.wait()


def body(fields, conductance, lateral, partition, arm_step, profiles, tile_ids, tile_count):
    tile = (8, 128)
    scratch = [
        (10, 128, 128), (8, 128, 128), (8, 128, 128), (3072, 128), (32, 9) + tile, (32, 3) + tile,
        (2, 8, 16, 128), (2, 8, 16, 128),
        (16, 3) + tile, (16, 2) + tile, (2, 16, 3) + tile, (2, 16, 2) + tile, (16, 3) + tile,
        (16, 3) + tile, (16, 2) + tile, (16, 3) + tile, (16, 2) + tile, (4, 3, 3) + tile,
        (4, 3) + tile, (4, 2) + tile, (4, 3) + tile, (4, 2) + tile, (4, 2) + tile, (4, 2) + tile,
        (16, 2) + tile, (16, 2) + tile, (2, 16, 2) + tile, (16, 2) + tile,
        (4, 16, 128), (3, 32, 64), (3, 64, 16), (3, 16, 128), (3, 32, 256), (3, 64, 256),
        (3, 512, 128), (3, 256, 128), (16, 384), (4, 256, 128),
    ]
    smem = pl.BlockSpec(memory_space=pltpu.SMEM)
    vmem = pl.BlockSpec(memory_space=pltpu.VMEM)
    hbm = pl.BlockSpec(memory_space=pl.ANY)
    new_fields, new_profiles = pl.pallas_call(
        functools.partial(kernel, lax.axis_size("xy")),
        out_shape=(
            jax.ShapeDtypeStruct((128, 1024), F32),
            jax.ShapeDtypeStruct((3072, 128), F32),
        ),
        in_specs=[hbm, hbm, smem, smem, vmem, hbm, smem, vmem, smem],
        out_specs=(hbm, hbm),
        scratch_shapes=[pltpu.VMEM(shape, F32) for shape in scratch]
        + [
            pltpu.SemaphoreType.DMA((16,)),
            pltpu.SemaphoreType.DMA((3,)),
            pltpu.SemaphoreType.DMA((16,)),
            pltpu.SemaphoreType.DMA((3,)),
            pltpu.SemaphoreType.DMA((32,)),
            pltpu.SemaphoreType.DMA((32,)),
        ],
        compiler_params=pltpu.CompilerParams(
            collective_id=0, has_side_effects=True, vmem_limit_bytes=40 * 2**20
        ),
        cost_estimate=pl.CostEstimate(flops=10**9, bytes_accessed=5 * 2**20, transcendentals=2048),
        name="ingot",
    )(
        fields.reshape(128, 1024), conductance.reshape(128, 1024), lateral, partition, arm_step,
        profiles.reshape(3072, 128), tile_ids, tile_ids, tile_count,
    )
    return new_fields.reshape(fields.shape), new_profiles.reshape(profiles.shape)


def solution(mesh):
    return jax.shard_map(
        body,
        mesh=mesh,
        in_specs=(
            P(None, "gz", "xy", None),
            P(None, "gz", "xy", None),
            P(),
            P(),
            P(),
            P(None, ("gz", "xy"), None, None),
            P(("gz", "xy"), None),
            P(("gz", "xy")),
        ),
        out_specs=(P(None, "gz", "xy", None), P(None, ("gz", "xy"), None, None)),
        check_vma=False,
    )
```

time: 409 us -> 61.4 us (0.15)
  waiting for transfers between devices: 207 us -> 0 us
  starting transfers between devices: 94.1 us -> 0 us
  other arithmetic: 56 us -> 0 us
  Pallas kernels: 0 us -> 51.5 us
  matrix products: 24.6 us -> 0 us
  local copies, waits for them, and re-layouts: 21.2 us -> 8.28 us
    ppermute x15 -> x0, waiting for transfers between devices: 207 us -> none  [the longest x13 207 us: from_behind(): return lax.ppermute(block, axis, route)]
    ppermute x15 -> x0, starting transfers between devices: 94.1 us -> none  [the longest x13 88.8 us: from_behind(): return lax.ppermute(block, axis, route)]
    pallas_call x0 -> x1, Pallas kernels: none -> 51.5 us  [body(): pl.pallas_call(functools.partial(kernel, lax.axis_size('xy')), out_shape=...]
    sub x3 -> x0, other arithmetic: 30.8 us -> none  [the longest x2 30.4 us: assemble(): back_rhs[row_at] - back_first[row_at] * first_value]
    dot_general x16 -> x0, matrix products: 24.6 us -> none  [substep(): jnp.einsum('jab,jsbc->jsac', arm_step, current, precision=lax.Precision.H...]
    div x14 -> x0, other arithmetic: 15.3 us -> none  [the longest x6 7.06 us: combine(): (current[2] - current[0] * below_rows[2] - current[1] * above_rows[2]) /...]
    concatenate x5 -> x0, local copies, waits for them, and re-layouts: 10.5 us -> none  [reduced_solve(): paired_rows = jnp.concatenate([first_row, last_row], axis=0)]
    unnamed x76 -> x16, local copies, waits for them, and re-layouts: 1.34 us -> 8.28 us
  transfers between devices with their start and end apart: 15 -> 0, of which waited for: 10 -> 0; matrix products, arithmetic and copies ran while one was open for 10% -> 0% of each run, Pallas kernels for 0% -> 0%
where the time goes in v1:
time: 61.4 us; the launch traced here: 61.1 us
  Pallas kernels  51.5 us (84%)
  local copies, waits for them, and re-layouts  8.28 us (13%)
  between operations  1.3 us (2%)
    pallas_call x1, Pallas kernels, body(): pl.pallas_call(functools.partial(kernel, lax.axis_size('xy')), out_shape=...  51.5 us
    unnamed x16, local copies, waits for them, and re-layouts  8.28 us

profile of v1, /device:TPU:1, one launch (start us, length us, event | category | flops | bytes accessed | tf_op | source)
XLA Modules:
  0.0 61.1 jit_solution(7989140370826998084)
XLA Ops:
  1.3 0.0 copy-start
  1.3 1.4 %copy-done = f32[3,16,64,128]{3,2,1,0:T(8,128)S(1)} copy-done((f32[3,16,64,128]{3,2,1,0:T(8,128)S(1)}, f32[3,16,64,128]{3,2,1,0:T(8,128)}, u32[]{:S(2)}) %copy-start) | copy-done | bytes 1572888
  2.7 0.0 copy-start.1
  2.7 1.0 %copy-done.1 = f32[4,4,8,1024]{3,2,1,0:T(8,128)S(1)} copy-done((f32[4,4,8,1024]{3,2,1,0:T(8,128)S(1)}, f32[4,4,8,1024]{3,2,1,0:T(8,128)}, u32[]{:S(2)}) %copy-start.1) | copy-done | bytes 524312
  3.7 0.0 copy-start.2
  3.7 1.0 %copy-done.2 = f32[4,4,8,1024]{3,2,1,0:T(8,128)S(1)} copy-done((f32[4,4,8,1024]{3,2,1,0:T(8,128)S(1)}, f32[4,4,8,1024]{3,2,1,0:T(8,128)}, u32[]{:S(2)}) %copy-start.2) | copy-done | bytes 524312
  4.8 0.0 copy-start.3
  4.8 0.9 %copy-done.3 = f32[3,64,64]{2,1,0:T(8,128)S(1)} copy-done((f32[3,64,64]{2,1,0:T(8,128)S(1)}, f32[3,64,64]{2,1,0:T(8,128)}, u32[]{:S(2)}) %copy-start.3) | copy-done | bytes 49176
  5.7 0.0 copy-start.4
  5.7 0.7 %copy-done.4 = f32[4]{0:T(128)S(1)} copy-done((f32[4]{0:T(128)S(1)}, f32[4]{0:T(128)}, u32[]{:S(2)}) %copy-start.4) | copy-done | bytes 40
  6.3 0.0 copy-start.5
  6.3 0.7 %copy-done.5 = f32[3]{0:T(128)S(1)} copy-done((f32[3]{0:T(128)S(1)}, f32[3]{0:T(128)}, u32[]{:S(2)}) %copy-start.5) | copy-done | bytes 36
  7.0 0.0 copy-start.6
  7.0 0.7 %copy-done.6 = s32[1,16]{1,0:T(1,128)S(1)} copy-done((s32[1,16]{1,0:T(1,128)S(1)}, s32[1,16]{1,0:T(1,128)}, u32[]{:S(2)}) %copy-start.6) | copy-done | bytes 88
  7.6 51.5 %ingot.1 = (f32[128,1024]{1,0:T(8,128)S(1)}, f32[3072,128]{1,0:T(8,128)S(1)}) custom-call(f32[128,1024]{1,0:T(8,128)S(1)} %bitcast.8, f32[128,1024]{1,0:T(8,128)S(1)} %bitcast.9, f32[4]{0:T(128)S(1)} %copy-done.4, f32[3]{0:T(128)S(1)} %copy-done.5, f32[3,64,64]{2,1,0:T(8,128)S(1)} %copy-done.3, f32[3072,128]{1,0:T(8,128)S(1)} %bitcast.7, ...), custom_call_target="tpu_custom_call" | custom-call | flops 1000000000 | bytes 5242880 | tf_op jit(solution)/shard_map/ingot/pallas_call | solution.py:506
  59.2 0.8 %copy.13 = f32[4,4,8,1024]{3,2,1,0:T(8,128)} copy(f32[4,4,8,1024]{3,2,1,0:T(8,128)S(1)} %bitcast.6) | data formatting | bytes 1048576
  59.9 1.1 %copy.14 = f32[3,16,64,128]{3,2,1,0:T(8,128)} copy(f32[3,16,64,128]{3,2,1,0:T(8,128)S(1)} %bitcast.5) | data formatting | bytes 3145728
Async XLA Ops:
  1.3 1.4 %copy-start = (f32[3,16,64,128]{3,2,1,0:T(8,128)S(1)}, f32[3,16,64,128]{3,2,1,0:T(8,128)}, u32[]{:S(2)}) copy-start(f32[3,16,64,128]{3,2,1,0:T(8,128)} %param.13) | copy-start | bytes 4718596
  2.7 1.0 %copy-start.1 = (f32[4,4,8,1024]{3,2,1,0:T(8,128)S(1)}, f32[4,4,8,1024]{3,2,1,0:T(8,128)}, u32[]{:S(2)}) copy-start(f32[4,4,8,1024]{3,2,1,0:T(8,128)} %param.8) | copy-start | bytes 1572868
  3.7 1.0 %copy-start.2 = (f32[4,4,8,1024]{3,2,1,0:T(8,128)S(1)}, f32[4,4,8,1024]{3,2,1,0:T(8,128)}, u32[]{:S(2)}) copy-start(f32[4,4,8,1024]{3,2,1,0:T(8,128)} %param.9) | copy-start | bytes 1572868
  4.8 0.9 %copy-start.3 = (f32[3,64,64]{2,1,0:T(8,128)S(1)}, f32[3,64,64]{2,1,0:T(8,128)}, u32[]{:S(2)}) copy-start(f32[3,64,64]{2,1,0:T(8,128)} %arm.1) | copy-start | bytes 147460
  5.7 0.7 %copy-start.4 = (f32[4]{0:T(128)S(1)}, f32[4]{0:T(128)}, u32[]{:S(2)}) copy-start(f32[4]{0:T(128)} %lateral.1) | copy-start | bytes 52
  6.3 0.7 %copy-start.5 = (f32[3]{0:T(128)S(1)}, f32[3]{0:T(128)}, u32[]{:S(2)}) copy-start(f32[3]{0:T(128)} %partition.1) | copy-start | bytes 40
  7.0 0.7 %copy-start.6 = (s32[1,16]{1,0:T(1,128)S(1)}, s32[1,16]{1,0:T(1,128)}, u32[]{:S(2)}) copy-start(s32[1,16]{1,0:T(1,128)} %ids_row.1) | copy-start | bytes 196

commit v2 on v1

--- a/solution.py
+++ b/solution.py
@@ -14,15 +14,8 @@
 SUB = 16
 ARM = 64
 SLOTS = 16
-DELTAS = (3, -3, 2, -2, 1, -1)
-
-ORDER = {}
-BASE = {}
-for _delta in (0,) + DELTAS:
-    BASE[_delta] = len(ORDER)
-    for _i in range(max(0, -_delta), min(4, 4 - _delta)):
-        ORDER[(_i, _i + _delta)] = len(ORDER)
-COUNT = {d: 4 - abs(d) for d in DELTAS}
+CHIPS = 16
+OFFSETS = (8, 7, 9, 6, 10, 5, 11, 4, 12, 3, 13, 2, 14, 1, 15)
 
 
 def merge_mass(low, high):
@@ -48,16 +41,15 @@
 
 def kernel(
     n_xy,
-    fields, cond, lateral, partition, arm, profiles, ids, ids_row, count,
+    fields, cond, lateral_in, partition_in, arm_in, profiles, ids_in, count,
     out_fields, out_profiles,
+    lateral, partition, ids, ids_row, arm,
     fld, cnd, src, prof, coef, tail,
     halo_s, halo_r,
     pair_cs, pair_rs, blk_c, blk_r, chip_coef,
-    l1_cs, l1_rs, l1_cr, l1_rr, sup_coef,
-    l2_cs, l2_rs, l2_cr, l2_rr, ret_s, ret_r,
-    back_s, back_r, fin, fin_r,
+    ring_cs, ring_rs, ring_cr, ring_rr, ret_s, ret_r, fin, fin_r, top_coef,
     cells, wsc, gsc, hsc, lhs1, lhs2, ysc, ssc, change, delta,
-    in_sem, prof_sem, out_sem, pout_sem,
+    in_sem, small_sem, prof_sem,
     send_sem, recv_sem,
 ):
     gz = lax.axis_index("gz")
@@ -65,11 +57,9 @@
     core = lax.rem(gz, 2)
     chip = gz // 2
     other = 1 - core
-    ring = chip // 4
-    phase = lax.rem(chip, 4)
 
     def at_chip(offset):
-        return (lax.rem(chip + (offset + 16), 16) * 2 + core, xy)
+        return (lax.rem(chip + offset, CHIPS) * 2 + core, xy)
 
     left = (gz, lax.rem(xy + n_xy - 1, n_xy))
     right = (gz, lax.rem(xy + 1, n_xy))
@@ -88,12 +78,17 @@
         )
         for j in range(3)
     ]
+    small = [(lateral_in, lateral), (partition_in, partition), (ids_in, ids)]
+    small += [(ids_in, ids_row), (arm_in, arm)]
+    small_loads = [
+        pltpu.make_async_copy(ref, buf, small_sem.at[n]) for n, (ref, buf) in enumerate(small)
+    ]
     barrier = pltpu.get_barrier_semaphore()
     partners = [left, right, peer]
-    partners += [at_chip(d) for d in DELTAS] + [at_chip(4 * d) for d in (1, 2, 3)]
+    partners += [at_chip(d) for d in OFFSETS]
     for partner in partners:
         pl.semaphore_signal(barrier, inc=1, device_id=partner, device_id_type=MESH)
-    for copy in field_loads + cond_loads + prof_loads:
+    for copy in field_loads + cond_loads + small_loads + prof_loads:
         copy.start()
 
     sends = []
@@ -117,12 +112,6 @@
     for y in range(8):
         halo_s[0, y] = fld[y + 1, pl.ds(0, 16, stride=8), :]
         halo_s[1, y] = fld[y + 1, pl.ds(7, 16, stride=8), :]
-    pl.semaphore_wait(barrier, len(partners))
-    halo = [
-        remote(halo_s.at[0], halo_r.at[1], left),
-        remote(halo_s.at[1], halo_r.at[0], right),
-    ]
-
     keep = jnp.where(gz == lax.axis_size("gz") - 1, 0.0, 1.0).astype(F32)
     for copy in cond_loads:
         copy.wait()
@@ -149,6 +138,11 @@
         for n in range(3):
             pair_cs[p, n] = block[n]
 
+    pl.semaphore_wait(barrier, len(partners))
+    halo = [
+        remote(halo_s.at[0], halo_r.at[1], left),
+        remote(halo_s.at[1], halo_r.at[0], right),
+    ]
     pair_c = remote(pair_cs, blk_c.at[core], peer)
 
     @pl.loop(0, 16, unroll=4)
@@ -157,6 +151,8 @@
         for n in range(3):
             blk_c[core, p, n] = block[n]
 
+    for copy in small_loads:
+        copy.wait()
     row = lax.broadcasted_iota(jnp.int32, (8, 128), 0)
     lane = lax.broadcasted_iota(jnp.int32, (8, 128), 1)
 
@@ -204,8 +200,14 @@
         lhs2[j, :, 224:240] = low
         lhs2[j, :, 240:256] = low
 
-    for j in range(3):
-        powers(j)
+    pair_c.wait_recv()
+    for d in range(CHIPS):
+        p = lax.rem(chip + d, CHIPS)
+        merged, held = merge_mass(*([blk_c[c, p, n] for n in range(3)] for c in range(2)))
+        for n in range(3):
+            chip_coef[d, n] = held[n]
+            ring_cs[d, n] = merged[n]
+    ring_c = [remote(ring_cs.at[d], ring_cr.at[CHIPS - d], at_chip(d)) for d in OFFSETS]
 
     for copy in halo:
         copy.wait_recv()
@@ -243,40 +245,20 @@
         for n in range(2):
             blk_r[core, p, n] = block[n]
 
-    def part_of(i, m):
-        return lax.rem(phase + 4 - i, 4) * 4 + m
-
-    pair_c.wait_recv()
-    for (i, m), s in ORDER.items():
-        p = part_of(i, m)
-        merged, held = merge_mass(*([blk_c[c, p, n] for n in range(3)] for c in range(2)))
-        target = l1_cr if i == m else l1_cs
-        for n in range(3):
-            chip_coef[s, n] = held[n]
-            target[s, n] = merged[n]
-
-    def spread(source, target, sign):
-        return [
-            remote(
-                source.at[pl.ds(BASE[d], COUNT[d])], target.at[pl.ds(BASE[d], COUNT[d])],
-                at_chip(sign * d),
-            )
-            for d in DELTAS
-        ]
-
-    l1_c = spread(l1_cs, l1_cr, 1)
     pair_r.wait_recv()
-    for (i, m), s in ORDER.items():
-        p = part_of(i, m)
-        merged, ratio = merge_rhs(
+    for d in range(CHIPS):
+        p = lax.rem(chip + d, CHIPS)
+        merged, chip_coef[d, 2] = merge_rhs(
             *([blk_r[c, p, n] for n in range(2)] for c in range(2)),
-            *(chip_coef[s, n] for n in range(3)),
+            *(chip_coef[d, n] for n in range(3)),
         )
-        chip_coef[s, 2] = ratio
-        target = l1_rr if i == m else l1_rs
         for n in range(2):
-            target[s, n] = merged[n]
-    l1_r = spread(l1_rs, l1_rr, 1)
+            ring_rs[d, n] = merged[n]
+    ring_r = [remote(ring_rs.at[d], ring_rr.at[CHIPS - d], at_chip(d)) for d in OFFSETS]
+
+    for j in range(3):
+        powers(j)
+
 
     for copy in prof_loads:
         copy.wait()
@@ -299,39 +281,6 @@
         y, at = lax.rem(tile, 8), (tile // 64) * 8 + lax.rem(tile // 8, 8)
         for f in range(4):
             cells[f, slot : slot + 1] = fld[y + 1, pl.ds(f * 32 + at, 1), :]
-
-    def group(buf, m, n_values):
-        return [[buf[ORDER[(i, m)], n] for n in range(n_values)] for i in range(4)]
-
-    def slot_of(m):
-        return lax.rem(m + 4 - ring, 4)
-
-    for copy in l1_c:
-        copy.wait_recv()
-    for m in range(4):
-        blocks = group(l1_cr, m, 3)
-        low, held1 = merge_mass(blocks[0], blocks[1])
-        high, held3 = merge_mass(blocks[2], blocks[3])
-        merged, held2 = merge_mass(low, high)
-        for k, held in enumerate((held1, held2, held3)):
-            for n in range(3):
-                sup_coef[m, k, n] = held[n]
-        for n in range(3):
-            l2_cs[slot_of(m), n] = merged[n]
-    l2_c = [remote(l2_cs.at[d], l2_cr.at[4 - d], at_chip(4 * d)) for d in (2, 1, 3)]
-    for copy in l1_r:
-        copy.wait_recv()
-    for m in range(4):
-        blocks = group(l1_rr, m, 2)
-        held = [[sup_coef[m, k, n] for n in range(3)] for k in range(3)]
-        low, ratio1 = merge_rhs(blocks[0], blocks[1], *held[0])
-        high, ratio3 = merge_rhs(blocks[2], blocks[3], *held[2])
-        merged, ratio2 = merge_rhs(low, high, *held[1])
-        for k, ratio in enumerate((ratio1, ratio2, ratio3)):
-            sup_coef[m, k, 2] = ratio
-        for n in range(2):
-            l2_rs[slot_of(m), n] = merged[n]
-    l2_r = [remote(l2_rs.at[d], l2_rr.at[4 - d], at_chip(4 * d)) for d in (2, 1, 3)]
 
     live = lax.broadcasted_iota(jnp.int32, (SLOTS, 128), 0) < count[0]
     solid = 0.9 / (1.0 + jnp.exp(cells[3]))
@@ -352,28 +301,44 @@
                 liquids.append(half * ((solute - fraction * mean) * inverses[k]))
                 ssc[j, pl.ds(SUB - 1 - k, SLOTS, stride=SUB), :] = liquids[k]
 
-    for copy in l2_c:
+    for copy in ring_c:
         copy.wait_recv()
-    masses = [[(l2_cr if b else l2_cs)[b, n] for n in range(3)] for b in range(4)]
-    low, held1 = merge_mass(masses[0], masses[1])
-    high, held3 = merge_mass(masses[2], masses[3])
-    whole, held2 = merge_mass(low, high)
-    for copy in l2_r:
+    masses = [[(ring_cr if b else ring_cs)[b, n] for n in range(3)] for b in range(CHIPS)]
+    levels = []
+    while len(masses) > 1:
+        joined = [merge_mass(*masses[b : b + 2]) for b in range(0, len(masses), 2)]
+        masses = [block for block, held in joined]
+        levels.append([held for block, held in joined])
+    for n, held in enumerate(held for level in levels for held in level):
+        for k in range(3):
+            top_coef[n, k] = held[k]
+    top_mass = masses[0][1] + masses[0][2]
+
+    for copy in ring_r:
         copy.wait_recv()
-    rhs = [[(l2_rr if b else l2_rs)[b, n] for n in range(2)] for b in range(4)]
-    low, ratio1 = merge_rhs(rhs[0], rhs[1], *held1)
-    high, ratio3 = merge_rhs(rhs[2], rhs[3], *held3)
-    total, ratio2 = merge_rhs(low, high, *held2)
-    v0 = (total[0] + total[1]) / (whole[1] + whole[2])
-    v2 = ratio2 + (held2[0] + held2[1]) * v0
-    v1 = ratio1 + held1[0] * v0 + held1[1] * v2
-    v3 = ratio3 + held3[0] * v2 + held3[1] * v0
-    values = [v0, v1, v2, v3, v0]
-    for b in range(4):
+    rhs = [[(ring_rr if b else ring_rs)[b, n] for n in range(2)] for b in range(CHIPS)]
+    levels, n = [], 0
+    while len(rhs) > 1:
+        level, joined = [], []
+        for b in range(0, len(rhs), 2):
+            a, c, inverse = (top_coef[n, k] for k in range(3))
+            block, ratio = merge_rhs(rhs[b], rhs[b + 1], a, c, inverse)
+            joined.append(block)
+            level.append((a, c, ratio))
+            n += 1
+        rhs = joined
+        levels.append(level)
+    values = [(rhs[0][0] + rhs[0][1]) / top_mass] * 2
+    for level in reversed(levels):
+        finer = [values[0]]
+        for b, (a, c, ratio) in enumerate(level):
+            finer += [ratio + a * values[b] + c * values[b + 1], values[b + 1]]
+        values = finer
+    for b in range(CHIPS):
         target = ret_s if b else ret_r
-        target[b, 0] = values[b]
-        target[b, 1] = values[b + 1]
-    ret = [remote(ret_s.at[b], ret_r.at[4 - b], at_chip(4 * b)) for b in (2, 1, 3)]
+        for n in range(2):
+            target[b, n] = values[b + n]
+    ret = [remote(ret_s.at[b], ret_r.at[CHIPS - b], at_chip(b)) for b in OFFSETS]
 
     def evolve(j):
         @pl.loop(0, 8)
@@ -392,36 +357,12 @@
             )
             for n in range(2):
                 shown = jnp.full((ARM, 128), 2 * t + n, jnp.int32) < count[0]
-                prof[pl.ds(at[n], 64), :] = jnp.where(
+                out_profiles[pl.ds(at[n], 64), :] = jnp.where(
                     shown, evolved[:, 128 * n : 128 * n + 128], 0.0
                 )
 
-        copy = pltpu.make_async_copy(
-            prof.at[pl.ds(1024 * j, 1024)], out_profiles.at[pl.ds(1024 * j, 1024)], pout_sem.at[j]
-        )
-        copy.start()
-        return copy
-
-    stores = [evolve(0)]
-
-    for copy in ret:
-        copy.wait_recv()
-    for m in range(4):
-        s = slot_of(m)
-        x0, x4 = ret_r[s, 0], ret_r[s, 1]
-        held = [[sup_coef[m, k, n] for n in range(3)] for k in range(3)]
-        x2 = held[1][2] + held[1][0] * x0 + held[1][1] * x4
-        x1 = held[0][2] + held[0][0] * x0 + held[0][1] * x2
-        x3 = held[2][2] + held[2][0] * x2 + held[2][1] * x4
-        values = [x0, x1, x2, x3, x4]
-        for i in range(4):
-            target = back_r if i == m else back_s
-            for n in range(2):
-                target[ORDER[(i, m)], n] = values[i + n]
-    back = spread(back_s, back_r, -1)
-
-    stores.append(evolve(1))
-    stores.append(evolve(2))
+    for j in range(3):
+        evolve(j)
 
     place = lax.broadcasted_iota(jnp.int32, (256, SLOTS), 0)
     named = (place // 64) * 64 + lax.rem(place, 8) * 8 + lax.rem(place // 8, 8)
@@ -437,12 +378,12 @@
         delta[j] = spreads[:, 128 * j : 128 * j + 128]
     delta[3] = jnp.zeros((256, 128), F32)
 
-    for copy in back:
+    for copy in ret:
         copy.wait_recv()
-    for (i, m), s in ORDER.items():
-        p = part_of(i, m)
-        low, high = back_r[s, 0], back_r[s, 1]
-        middle = chip_coef[s, 2] + chip_coef[s, 0] * low + chip_coef[s, 1] * high
+    for d in range(CHIPS):
+        p = lax.rem(chip + d, CHIPS)
+        low, high = ret_r[d, 0], ret_r[d, 1]
+        middle = chip_coef[d, 2] + chip_coef[d, 0] * low + chip_coef[d, 1] * high
         fin[0, p, 0] = low
         fin[0, p, 1] = middle
         fin[1, p, 0] = middle
@@ -457,34 +398,35 @@
         for z in (3, 2, 1):
             above = tail[e, z - 1] + coef[e, 3 * z - 3] * low + coef[e, 3 * z - 2] * above
             values[z] = above
+        lanes = pl.ds(pl.multiple_of(y * 128, 128), 128)
         for z in range(4):
             at = pl.ds(pl.multiple_of(f * 32 + z * 8, 8), 8)
-            src[y, at, :] = values[z] + delta[f, pl.ds(pl.multiple_of(z * 64 + y * 8, 8), 8), :]
-
-    def store(owner, n):
-        for y in range(8):
-            rows = pl.ds(pl.multiple_of(owner * 64, 64), 64)
-            copy = pltpu.make_async_copy(
-                src.at[y, rows], out_fields.at[rows, pl.ds(128 * y, 128)], out_sem.at[n + y]
-            )
-            copy.start()
-            stores.append(copy)
+            out_fields[at, lanes] = values[z] + delta[f, pl.ds(pl.multiple_of(z * 64 + y * 8, 8), 8), :]
 
     @pl.loop(0, 16, unroll=4)
     def _(p):
         finish(core, p, fin[core, p, 0], fin[core, p, 1])
 
-    store(core, 0)
     last.wait_recv()
 
     @pl.loop(0, 16, unroll=4)
     def _(p):
         finish(other, p, fin_r[p, 0], fin_r[p, 1])
 
-    store(other, 8)
     for copy in sends:
         copy.wait_send()
-    for copy in stores:
+
+
+def deliver(new_fields, new_profiles, out_fields, out_profiles, sem):
+    copies = [pltpu.make_async_copy(new_fields, out_fields, sem.at[0])]
+    for n in range(3):
+        rows = pl.ds(1024 * n, 1024)
+        copies.append(
+            pltpu.make_async_copy(new_profiles.at[rows], out_profiles.at[rows], sem.at[n + 1])
+        )
+    for copy in copies:
+        copy.start()
+    for copy in copies:
         copy.wait()
 
 
@@ -494,40 +436,55 @@
         (10, 128, 128), (8, 128, 128), (8, 128, 128), (3072, 128), (32, 9) + tile, (32, 3) + tile,
         (2, 8, 16, 128), (2, 8, 16, 128),
         (16, 3) + tile, (16, 2) + tile, (2, 16, 3) + tile, (2, 16, 2) + tile, (16, 3) + tile,
-        (16, 3) + tile, (16, 2) + tile, (16, 3) + tile, (16, 2) + tile, (4, 3, 3) + tile,
-        (4, 3) + tile, (4, 2) + tile, (4, 3) + tile, (4, 2) + tile, (4, 2) + tile, (4, 2) + tile,
-        (16, 2) + tile, (16, 2) + tile, (2, 16, 2) + tile, (16, 2) + tile,
+        (16, 3) + tile, (16, 2) + tile, (16, 3) + tile, (16, 2) + tile, (16, 2) + tile, (16, 2) + tile,
+        (2, 16, 2) + tile, (16, 2) + tile, (15, 3) + tile,
         (4, 16, 128), (3, 32, 64), (3, 64, 16), (3, 16, 128), (3, 32, 256), (3, 64, 256),
         (3, 512, 128), (3, 256, 128), (16, 384), (4, 256, 128),
     ]
-    smem = pl.BlockSpec(memory_space=pltpu.SMEM)
+    hbm = pl.BlockSpec(memory_space=pl.ANY)
     vmem = pl.BlockSpec(memory_space=pltpu.VMEM)
-    hbm = pl.BlockSpec(memory_space=pl.ANY)
+    operands = [
+        pltpu.with_memory_space_constraint(x, pltpu.HBM)
+        for x in (
+            fields.reshape(128, 1024), conductance.reshape(128, 1024), lateral, partition,
+            arm_step, profiles.reshape(3072, 128), tile_ids,
+        )
+    ]
     new_fields, new_profiles = pl.pallas_call(
         functools.partial(kernel, lax.axis_size("xy")),
-        out_shape=(
-            jax.ShapeDtypeStruct((128, 1024), F32),
-            jax.ShapeDtypeStruct((3072, 128), F32),
-        ),
-        in_specs=[hbm, hbm, smem, smem, vmem, hbm, smem, vmem, smem],
-        out_specs=(hbm, hbm),
-        scratch_shapes=[pltpu.VMEM(shape, F32) for shape in scratch]
+        out_shape=(pltpu.VMEM((128, 1024), F32), pltpu.VMEM((3072, 128), F32)),
+        in_specs=[hbm] * 7 + [pl.BlockSpec(memory_space=pltpu.SMEM)],
+        out_specs=(vmem, vmem),
+        scratch_shapes=[
+            pltpu.SMEM((4,), F32), pltpu.SMEM((3,), F32),
+            pltpu.SMEM((1, SLOTS), jnp.int32),
+            pltpu.VMEM((1, SLOTS), jnp.int32), pltpu.VMEM((3, ARM, ARM), F32),
+        ]
+        + [pltpu.VMEM(shape, F32) for shape in scratch]
         + [
             pltpu.SemaphoreType.DMA((16,)),
+            pltpu.SemaphoreType.DMA((5,)),
             pltpu.SemaphoreType.DMA((3,)),
-            pltpu.SemaphoreType.DMA((16,)),
-            pltpu.SemaphoreType.DMA((3,)),
-            pltpu.SemaphoreType.DMA((32,)),
-            pltpu.SemaphoreType.DMA((32,)),
+            pltpu.SemaphoreType.DMA((50,)),
+            pltpu.SemaphoreType.DMA((50,)),
         ],
         compiler_params=pltpu.CompilerParams(
             collective_id=0, has_side_effects=True, vmem_limit_bytes=40 * 2**20
         ),
         cost_estimate=pl.CostEstimate(flops=10**9, bytes_accessed=5 * 2**20, transcendentals=2048),
         name="ingot",
+    )(*operands, tile_count)
+    new_fields, new_profiles = pl.pallas_call(
+        deliver,
+        out_shape=(pltpu.HBM((128, 1024), F32), pltpu.HBM((3072, 128), F32)),
+        in_specs=[vmem, vmem],
+        out_specs=(hbm, hbm),
+        scratch_shapes=[pltpu.SemaphoreType.DMA((4,))],
+        cost_estimate=pl.CostEstimate(flops=0, bytes_accessed=2**22, transcendentals=0),
+        name="deliver",
     )(
-        fields.reshape(128, 1024), conductance.reshape(128, 1024), lateral, partition, arm_step,
-        profiles.reshape(3072, 128), tile_ids, tile_ids, tile_count,
+        pltpu.with_memory_space_constraint(new_fields, pltpu.VMEM),
+        pltpu.with_memory_space_constraint(new_profiles, pltpu.VMEM),
     )
     return new_fields.reshape(fields.shape), new_profiles.reshape(profiles.shape)
 

time: 61.4 us -> 47.9 us (0.78)
  local copies, waits for them, and re-layouts: 8.28 us -> 0 us
  Pallas kernels: 51.5 us -> 46.4 us
    unnamed x16 -> x0, local copies, waits for them, and re-layouts: 8.28 us -> none
    pallas_call x1, Pallas kernels: 51.5 us -> 45.1 us  [body(): pl.pallas_call(functools.partial(kernel, lax.axis_size('xy')), out_shape=...]
    pallas_call x0 -> x1, Pallas kernels: none -> 1.35 us  [body(): pl.pallas_call(deliver, out_shape=(pltpu.HBM((128, 1024), F32), pltpu.HBM...]
where the time goes in v2:
time: 47.9 us; the launch traced here: 47.7 us
  Pallas kernels  46.4 us (97%)
  between operations  1.29 us (3%)
    pallas_call x1, Pallas kernels, body(): pl.pallas_call(functools.partial(kernel, lax.axis_size('xy')), out_shape=...  45.1 us
    pallas_call x1, Pallas kernels, body(): pl.pallas_call(deliver, out_shape=(pltpu.HBM((128, 1024), F32), pltpu.HBM...  1.35 us

profile of v2, /device:TPU:1, one launch (start us, length us, event | category | flops | bytes accessed | tf_op | source)
XLA Modules:
  0.0 47.7 jit_solution(12482396843745875334)
XLA Ops:
  1.3 45.1 %ingot.1 = (f32[128,1024]{1,0:T(8,128)S(1)}, f32[3072,128]{1,0:T(8,128)S(1)}) custom-call(f32[128,1024]{1,0:T(8,128)} %bitcast.7, f32[128,1024]{1,0:T(8,128)} %bitcast.8, f32[4]{0:T(128)} %lateral_in.1, f32[3]{0:T(128)} %partition_in.1, f32[3,64,64]{2,1,0:T(8,128)} %arm_in.1, f32[3072,128]{1,0:T(8,128)} %bitcast.5, s32[1,16]{1,0:T(1,128)} %ids_in.1, ...), custom_call_target="tpu_custom_call" | custom-call | flops 1000000000 | bytes 5242880 | tf_op jit(solution)/shard_map/ingot/pallas_call | solution.py:453
  46.4 1.3 %deliver.1 = (f32[128,1024]{1,0:T(8,128)}, f32[3072,128]{1,0:T(8,128)}) custom-call(f32[128,1024]{1,0:T(8,128)S(1)} %get-tuple-element.6.new_fields, f32[3072,128]{1,0:T(8,128)S(1)} %get-tuple-element.7.new_profiles), custom_call_target="tpu_custom_call" | custom-call | bytes 4194304 | tf_op jit(solution)/shard_map/deliver/pallas_call | solution.py:477

commit v3 on v2

--- a/solution.py
+++ b/solution.py
@@ -15,7 +15,10 @@
 ARM = 64
 SLOTS = 16
 CHIPS = 16
-OFFSETS = (8, 7, 9, 6, 10, 5, 11, 4, 12, 3, 13, 2, 14, 1, 15)
+HALF = CHIPS // 2
+REACH = 5
+TO = [REACH - i for i in range(HALF)] + [2 * REACH - i for i in range(HALF, CHIPS)]
+SENT = sorted((i for i in range(CHIPS) if TO[i]), key=lambda i: (-abs(TO[i]), i))
 
 
 def merge_mass(low, high):
@@ -47,7 +50,8 @@
     fld, cnd, src, prof, coef, tail,
     halo_s, halo_r,
     pair_cs, pair_rs, blk_c, blk_r, chip_coef,
-    ring_cs, ring_rs, ring_cr, ring_rr, ret_s, ret_r, fin, fin_r, top_coef,
+    ring_cs, ring_rs, ring_cr, ring_rr, half_cs, half_rs, half_cr, half_rr,
+    ret_s, ret_r, fin, fin_r, top_coef,
     cells, wsc, gsc, hsc, lhs1, lhs2, ysc, ssc, change, delta,
     in_sem, small_sem, prof_sem,
     send_sem, recv_sem,
@@ -59,7 +63,7 @@
     other = 1 - core
 
     def at_chip(offset):
-        return (lax.rem(chip + offset, CHIPS) * 2 + core, xy)
+        return (lax.rem(chip + (offset + CHIPS), CHIPS) * 2 + core, xy)
 
     left = (gz, lax.rem(xy + n_xy - 1, n_xy))
     right = (gz, lax.rem(xy + 1, n_xy))
@@ -84,8 +88,17 @@
         pltpu.make_async_copy(ref, buf, small_sem.at[n]) for n, (ref, buf) in enumerate(small)
     ]
     barrier = pltpu.get_barrier_semaphore()
-    partners = [left, right, peer]
-    partners += [at_chip(d) for d in OFFSETS]
+    has_left, has_right = xy > 0, xy < n_xy - 1
+
+    @pl.when(has_left)
+    def _():
+        pl.semaphore_signal(barrier, inc=1, device_id=left, device_id_type=MESH)
+
+    @pl.when(has_right)
+    def _():
+        pl.semaphore_signal(barrier, inc=1, device_id=right, device_id_type=MESH)
+
+    partners = [peer] + [at_chip(d * sign) for d in range(1, REACH + 1) for sign in (1, -1)]
     for partner in partners:
         pl.semaphore_signal(barrier, inc=1, device_id=partner, device_id_type=MESH)
     for copy in field_loads + cond_loads + small_loads + prof_loads:
@@ -94,13 +107,16 @@
     sends = []
     used = [0]
 
-    def remote(source, target, device):
+    def describe(source, target, device):
         n = used[0]
         used[0] = n + 1
-        copy = pltpu.make_async_remote_copy(
+        return pltpu.make_async_remote_copy(
             src_ref=source, dst_ref=target, send_sem=send_sem.at[n], recv_sem=recv_sem.at[n],
             device_id=device, device_id_type=MESH,
         )
+
+    def remote(source, target, device):
+        copy = describe(source, target, device)
         copy.start()
         sends.append(copy)
         return copy
@@ -138,11 +154,16 @@
         for n in range(3):
             pair_cs[p, n] = block[n]
 
-    pl.semaphore_wait(barrier, len(partners))
-    halo = [
-        remote(halo_s.at[0], halo_r.at[1], left),
-        remote(halo_s.at[1], halo_r.at[0], right),
-    ]
+    edges = lax.min(xy, 1) + lax.min(n_xy - 1 - xy, 1)
+    pl.semaphore_wait(barrier, len(partners) + edges)
+    to_left = describe(halo_s.at[0], halo_r.at[1], left)
+    to_right = describe(halo_s.at[1], halo_r.at[0], right)
+    sides = ((has_left, to_left, to_right, 0), (has_right, to_right, to_left, 1))
+    for present, outward, unused, unused_side in sides:
+        @pl.when(present)
+        def _(outward=outward):
+            outward.start()
+
     pair_c = remote(pair_cs, blk_c.at[core], peer)
 
     @pl.loop(0, 16, unroll=4)
@@ -150,24 +171,6 @@
         block = eliminate_mass(core, p)
         for n in range(3):
             blk_c[core, p, n] = block[n]
-
-    for copy in small_loads:
-        copy.wait()
-    row = lax.broadcasted_iota(jnp.int32, (8, 128), 0)
-    lane = lax.broadcasted_iota(jnp.int32, (8, 128), 1)
-
-    @pl.loop(0, 16)
-    def _(q):
-        at = pl.ds(pl.multiple_of(q * 8, 8), 8)
-        rate = lateral[q // 4]
-        tiles = [fld[y, at, :] for y in range(10)]
-        for y in range(8):
-            before, here, after = tiles[y : y + 3]
-            down = jnp.where(row == 0, 0.0, pltpu.roll(here, 1, 0))
-            up = jnp.where(row == 7, 0.0, pltpu.roll(here, 7, 0))
-            low = pltpu.roll(jnp.where(lane == 127, before, here), 1, 1)
-            high = pltpu.roll(jnp.where(lane == 0, after, here), 127, 1)
-            src[y, at, :] = here + rate * (down + up + low + high - 4.0 * here)
 
     def powers(j):
         power = arm[j]
@@ -200,19 +203,45 @@
         lhs2[j, :, 224:240] = low
         lhs2[j, :, 240:256] = low
 
+    def part_at(i):
+        return lax.rem(chip + (CHIPS - i), CHIPS)
+
     pair_c.wait_recv()
-    for d in range(CHIPS):
-        p = lax.rem(chip + d, CHIPS)
+    for i in range(CHIPS):
+        p = part_at(i)
         merged, held = merge_mass(*([blk_c[c, p, n] for n in range(3)] for c in range(2)))
+        target = ring_cs if TO[i] else ring_cr
         for n in range(3):
-            chip_coef[d, n] = held[n]
-            ring_cs[d, n] = merged[n]
-    ring_c = [remote(ring_cs.at[d], ring_cr.at[CHIPS - d], at_chip(d)) for d in OFFSETS]
-
-    for copy in halo:
-        copy.wait_recv()
-    first = jnp.where(xy == 0, 0.0, 1.0).astype(F32)
-    final = jnp.where(xy == n_xy - 1, 0.0, 1.0).astype(F32)
+            chip_coef[i, n] = held[n]
+            target[i, n] = merged[n]
+    ring_c = [remote(ring_cs.at[i], ring_cr.at[i], at_chip(TO[i])) for i in SENT]
+
+    for copy in small_loads:
+        copy.wait()
+    row = lax.broadcasted_iota(jnp.int32, (8, 128), 0)
+    lane = lax.broadcasted_iota(jnp.int32, (8, 128), 1)
+
+    @pl.loop(0, 16)
+    def _(q):
+        at = pl.ds(pl.multiple_of(q * 8, 8), 8)
+        rate = lateral[q // 4]
+        tiles = [fld[y, at, :] for y in range(10)]
+        for y in range(8):
+            before, here, after = tiles[y : y + 3]
+            down = jnp.where(row == 0, 0.0, pltpu.roll(here, 1, 0))
+            up = jnp.where(row == 7, 0.0, pltpu.roll(here, 7, 0))
+            low = pltpu.roll(jnp.where(lane == 127, before, here), 1, 1)
+            high = pltpu.roll(jnp.where(lane == 0, after, here), 127, 1)
+            src[y, at, :] = here + rate * (down + up + low + high - 4.0 * here)
+
+    for present, unused, inward, side in sides:
+        @pl.when(present)
+        def _(inward=inward):
+            inward.wait_recv()
+
+        @pl.when(jnp.logical_not(present))
+        def _(side=side):
+            halo_r[side] = jnp.zeros((8, 16, 128), F32)
 
     def eliminate_rhs(owner, p):
         f, y = owner * 2 + p // 8, lax.rem(p, 8)
@@ -220,8 +249,8 @@
         rate = lateral[f]
         block = None
         for z in range(4):
-            edge = jnp.where(row == 0, halo_r[0, y, pl.ds(f * 4 + z, 1), :] * (rate * first), 0.0)
-            edge += jnp.where(row == 7, halo_r[1, y, pl.ds(f * 4 + z, 1), :] * (rate * final), 0.0)
+            edge = jnp.where(row == 0, halo_r[0, y, pl.ds(f * 4 + z, 1), :] * rate, 0.0)
+            edge += jnp.where(row == 7, halo_r[1, y, pl.ds(f * 4 + z, 1), :] * rate, 0.0)
             here = plane(src, y, f, z) + edge
             if z == 0:
                 block = (here, 0.0)
@@ -246,19 +275,37 @@
             blk_r[core, p, n] = block[n]
 
     pair_r.wait_recv()
-    for d in range(CHIPS):
-        p = lax.rem(chip + d, CHIPS)
-        merged, chip_coef[d, 2] = merge_rhs(
+    for i in range(CHIPS):
+        p = part_at(i)
+        merged, chip_coef[i, 2] = merge_rhs(
             *([blk_r[c, p, n] for n in range(2)] for c in range(2)),
-            *(chip_coef[d, n] for n in range(3)),
+            *(chip_coef[i, n] for n in range(3)),
         )
+        target = ring_rs if TO[i] else ring_rr
         for n in range(2):
-            ring_rs[d, n] = merged[n]
-    ring_r = [remote(ring_rs.at[d], ring_rr.at[CHIPS - d], at_chip(d)) for d in OFFSETS]
+            target[i, n] = merged[n]
+    ring_r = [remote(ring_rs.at[i], ring_rr.at[i], at_chip(TO[i])) for i in SENT]
 
     for j in range(3):
         powers(j)
 
+
+    for copy in ring_c:
+        copy.wait_recv()
+    for half in range(2):
+        masses = [[ring_cr[half * HALF + b, n] for n in range(3)] for b in range(HALF)]
+        at = 0
+        while len(masses) > 1:
+            joined = [merge_mass(*masses[b : b + 2]) for b in range(0, len(masses), 2)]
+            masses = [block for block, held in joined]
+            for block, held in joined:
+                for n in range(3):
+                    top_coef[half, at, n] = held[n]
+                at += 1
+        for n in range(3):
+            half_cs[half, n] = masses[0][n]
+    across = (at_chip(REACH), at_chip(-REACH))
+    half_c = [remote(half_cs.at[h], half_cr.at[1 - h], across[h]) for h in range(2)]
 
     for copy in prof_loads:
         copy.wait()
@@ -301,44 +348,26 @@
                 liquids.append(half * ((solute - fraction * mean) * inverses[k]))
                 ssc[j, pl.ds(SUB - 1 - k, SLOTS, stride=SUB), :] = liquids[k]
 
-    for copy in ring_c:
-        copy.wait_recv()
-    masses = [[(ring_cr if b else ring_cs)[b, n] for n in range(3)] for b in range(CHIPS)]
-    levels = []
-    while len(masses) > 1:
-        joined = [merge_mass(*masses[b : b + 2]) for b in range(0, len(masses), 2)]
-        masses = [block for block, held in joined]
-        levels.append([held for block, held in joined])
-    for n, held in enumerate(held for level in levels for held in level):
-        for k in range(3):
-            top_coef[n, k] = held[k]
-    top_mass = masses[0][1] + masses[0][2]
-
     for copy in ring_r:
         copy.wait_recv()
-    rhs = [[(ring_rr if b else ring_rs)[b, n] for n in range(2)] for b in range(CHIPS)]
-    levels, n = [], 0
-    while len(rhs) > 1:
-        level, joined = [], []
-        for b in range(0, len(rhs), 2):
-            a, c, inverse = (top_coef[n, k] for k in range(3))
-            block, ratio = merge_rhs(rhs[b], rhs[b + 1], a, c, inverse)
-            joined.append(block)
-            level.append((a, c, ratio))
-            n += 1
-        rhs = joined
-        levels.append(level)
-    values = [(rhs[0][0] + rhs[0][1]) / top_mass] * 2
-    for level in reversed(levels):
-        finer = [values[0]]
-        for b, (a, c, ratio) in enumerate(level):
-            finer += [ratio + a * values[b] + c * values[b + 1], values[b + 1]]
-        values = finer
-    for b in range(CHIPS):
-        target = ret_s if b else ret_r
+    levels = ([], [])
+    for half in range(2):
+        rhs = [[ring_rr[half * HALF + b, n] for n in range(2)] for b in range(HALF)]
+        at = 0
+        while len(rhs) > 1:
+            level, joined = [], []
+            for b in range(0, len(rhs), 2):
+                block, top_coef[half, at, 2] = merge_rhs(
+                    rhs[b], rhs[b + 1], *(top_coef[half, at, n] for n in range(3))
+                )
+                joined.append(block)
+                level.append(at)
+                at += 1
+            rhs = joined
+            levels[half].append(level)
         for n in range(2):
-            target[b, n] = values[b + n]
-    ret = [remote(ret_s.at[b], ret_r.at[CHIPS - b], at_chip(b)) for b in OFFSETS]
+            half_rs[half, n] = rhs[0][n]
+    half_r = [remote(half_rs.at[h], half_rr.at[1 - h], across[h]) for h in range(2)]
 
     def evolve(j):
         @pl.loop(0, 8)
@@ -361,8 +390,35 @@
                     shown, evolved[:, 128 * n : 128 * n + 128], 0.0
                 )
 
-    for j in range(3):
-        evolve(j)
+    evolve(0)
+
+    for copy in half_c + half_r:
+        copy.wait_recv()
+    for half in range(2):
+        own, met = (half_cs, half_rs), (half_cr, half_rr)
+        lower, upper = (own, met) if half == 0 else (met, own)
+        whole, held = merge_mass(*([buf[0][half, n] for n in range(3)] for buf in (lower, upper)))
+        total, ratio = merge_rhs(
+            *([buf[1][half, n] for n in range(2)] for buf in (lower, upper)), *held
+        )
+        start = (total[0] + total[1]) / (whole[1] + whole[2])
+        middle = ratio + (held[0] + held[1]) * start
+        values = [start, middle] if half == 0 else [middle, start]
+        for level in reversed(levels[half]):
+            finer = [values[0]]
+            for b, at in enumerate(level):
+                a, c, ratio = (top_coef[half, at, n] for n in range(3))
+                finer += [ratio + a * values[b] + c * values[b + 1], values[b + 1]]
+            values = finer
+        for b in range(HALF):
+            i = half * HALF + b
+            target = ret_s if TO[i] else ret_r
+            for n in range(2):
+                target[i, n] = values[b + n]
+    ret = [remote(ret_s.at[i], ret_r.at[i], at_chip(-TO[i])) for i in SENT]
+
+    evolve(1)
+    evolve(2)
 
     place = lax.broadcasted_iota(jnp.int32, (256, SLOTS), 0)
     named = (place // 64) * 64 + lax.rem(place, 8) * 8 + lax.rem(place // 8, 8)
@@ -380,10 +436,10 @@
 
     for copy in ret:
         copy.wait_recv()
-    for d in range(CHIPS):
-        p = lax.rem(chip + d, CHIPS)
-        low, high = ret_r[d, 0], ret_r[d, 1]
-        middle = chip_coef[d, 2] + chip_coef[d, 0] * low + chip_coef[d, 1] * high
+    for i in range(CHIPS):
+        p = part_at(i)
+        low, high = ret_r[i, 0], ret_r[i, 1]
+        middle = chip_coef[i, 2] + chip_coef[i, 0] * low + chip_coef[i, 1] * high
         fin[0, p, 0] = low
         fin[0, p, 1] = middle
         fin[1, p, 0] = middle
@@ -413,17 +469,23 @@
     def _(p):
         finish(other, p, fin_r[p, 0], fin_r[p, 1])
 
+    for present, outward, unused, unused_side in sides:
+        @pl.when(present)
+        def _(outward=outward):
+            outward.wait_send()
+
     for copy in sends:
         copy.wait_send()
 
 
 def deliver(new_fields, new_profiles, out_fields, out_profiles, sem):
-    copies = [pltpu.make_async_copy(new_fields, out_fields, sem.at[0])]
-    for n in range(3):
-        rows = pl.ds(1024 * n, 1024)
-        copies.append(
-            pltpu.make_async_copy(new_profiles.at[rows], out_profiles.at[rows], sem.at[n + 1])
-        )
+    copies = []
+    for ref, out, rows, pieces in (
+        (new_profiles, out_profiles, 512, 6), (new_fields, out_fields, 64, 2),
+    ):
+        for n in range(pieces):
+            part = pl.ds(rows * n, rows)
+            copies.append(pltpu.make_async_copy(ref.at[part], out.at[part], sem.at[len(copies)]))
     for copy in copies:
         copy.start()
     for copy in copies:
@@ -436,8 +498,9 @@
         (10, 128, 128), (8, 128, 128), (8, 128, 128), (3072, 128), (32, 9) + tile, (32, 3) + tile,
         (2, 8, 16, 128), (2, 8, 16, 128),
         (16, 3) + tile, (16, 2) + tile, (2, 16, 3) + tile, (2, 16, 2) + tile, (16, 3) + tile,
-        (16, 3) + tile, (16, 2) + tile, (16, 3) + tile, (16, 2) + tile, (16, 2) + tile, (16, 2) + tile,
-        (2, 16, 2) + tile, (16, 2) + tile, (15, 3) + tile,
+        (16, 3) + tile, (16, 2) + tile, (16, 3) + tile, (16, 2) + tile,
+        (2, 3) + tile, (2, 2) + tile, (2, 3) + tile, (2, 2) + tile,
+        (16, 2) + tile, (16, 2) + tile, (2, 16, 2) + tile, (16, 2) + tile, (2, 7, 3) + tile,
         (4, 16, 128), (3, 32, 64), (3, 64, 16), (3, 16, 128), (3, 32, 256), (3, 64, 256),
         (3, 512, 128), (3, 256, 128), (16, 384), (4, 256, 128),
     ]
@@ -465,8 +528,8 @@
             pltpu.SemaphoreType.DMA((16,)),
             pltpu.SemaphoreType.DMA((5,)),
             pltpu.SemaphoreType.DMA((3,)),
-            pltpu.SemaphoreType.DMA((50,)),
-            pltpu.SemaphoreType.DMA((50,)),
+            pltpu.SemaphoreType.DMA((51,)),
+            pltpu.SemaphoreType.DMA((51,)),
         ],
         compiler_params=pltpu.CompilerParams(
             collective_id=0, has_side_effects=True, vmem_limit_bytes=40 * 2**20
@@ -479,7 +542,7 @@
         out_shape=(pltpu.HBM((128, 1024), F32), pltpu.HBM((3072, 128), F32)),
         in_specs=[vmem, vmem],
         out_specs=(hbm, hbm),
-        scratch_shapes=[pltpu.SemaphoreType.DMA((4,))],
+        scratch_shapes=[pltpu.SemaphoreType.DMA((8,))],
         cost_estimate=pl.CostEstimate(flops=0, bytes_accessed=2**22, transcendentals=0),
         name="deliver",
     )(

time: 47.9 us -> 42.8 us (0.89)
  Pallas kernels: 46.4 us -> 41.4 us
    pallas_call x1, Pallas kernels: 45.1 us -> 40 us  [body(): pl.pallas_call(functools.partial(kernel, lax.axis_size('xy')), out_shape=...]
where the time goes in v3:
time: 42.8 us; the launch traced here: 42.7 us
  Pallas kernels  41.4 us (97%)
  between operations  1.29 us (3%)
    pallas_call x1, Pallas kernels, body(): pl.pallas_call(functools.partial(kernel, lax.axis_size('xy')), out_shape=...  40 us
    pallas_call x1, Pallas kernels, body(): pl.pallas_call(deliver, out_shape=(pltpu.HBM((128, 1024), F32), pltpu.HBM...  1.38 us

profile of v3, /device:TPU:1, one launch (start us, length us, event | category | flops | bytes accessed | tf_op | source)
XLA Modules:
  0.0 42.7 jit_solution(10868552307127767888)
XLA Ops:
  1.3 40.0 %ingot.1 = (f32[128,1024]{1,0:T(8,128)S(1)}, f32[3072,128]{1,0:T(8,128)S(1)}) custom-call(f32[128,1024]{1,0:T(8,128)} %bitcast.7, f32[128,1024]{1,0:T(8,128)} %bitcast.8, f32[4]{0:T(128)} %lateral_in.1, f32[3]{0:T(128)} %partition_in.1, f32[3,64,64]{2,1,0:T(8,128)} %arm_in.1, f32[3072,128]{1,0:T(8,128)} %bitcast.5, s32[1,16]{1,0:T(1,128)} %ids_in.1, ...), custom_call_target="tpu_custom_call" | custom-call | flops 1000000000 | bytes 5242880 | tf_op jit(solution)/shard_map/ingot/pallas_call | solution.py:516
  41.3 1.4 %deliver.1 = (f32[128,1024]{1,0:T(8,128)}, f32[3072,128]{1,0:T(8,128)}) custom-call(f32[128,1024]{1,0:T(8,128)S(1)} %get-tuple-element.6.new_fields, f32[3072,128]{1,0:T(8,128)S(1)} %get-tuple-element.7.new_profiles), custom_call_target="tpu_custom_call" | custom-call | bytes 4194304 | tf_op jit(solution)/shard_map/deliver/pallas_call | solution.py:540

commit v4 on v3

--- a/solution.py
+++ b/solution.py
@@ -17,8 +17,12 @@
 CHIPS = 16
 HALF = CHIPS // 2
 REACH = 5
+KNOWN = 3
 TO = [REACH - i for i in range(HALF)] + [2 * REACH - i for i in range(HALF, CHIPS)]
-SENT = sorted((i for i in range(CHIPS) if TO[i]), key=lambda i: (-abs(TO[i]), i))
+PLACES = sorted(range(CHIPS), key=lambda i: (-abs(TO[i]), i))
+SENT = PLACES[:-2]
+OUT = ((0, 4), (4, 8), (8, 12), (12, 16))
+BACK = ((10, 16), (4, 10), (0, 4))
 
 
 def merge_mass(low, high):
@@ -54,7 +58,7 @@
     ret_s, ret_r, fin, fin_r, top_coef,
     cells, wsc, gsc, hsc, lhs1, lhs2, ysc, ssc, change, delta,
     in_sem, small_sem, prof_sem,
-    send_sem, recv_sem,
+    send_sem, recv_sem, near_sem,
 ):
     gz = lax.axis_index("gz")
     xy = lax.axis_index("xy")
@@ -90,6 +94,9 @@
     barrier = pltpu.get_barrier_semaphore()
     has_left, has_right = xy > 0, xy < n_xy - 1
 
+    partners = [at_chip(d * sign) for d in range(KNOWN, 0, -1) for sign in (1, -1)] + [peer]
+    for partner in partners:
+        pl.semaphore_signal(barrier, inc=1, device_id=partner, device_id_type=MESH)
     @pl.when(has_left)
     def _():
         pl.semaphore_signal(barrier, inc=1, device_id=left, device_id_type=MESH)
@@ -98,10 +105,7 @@
     def _():
         pl.semaphore_signal(barrier, inc=1, device_id=right, device_id_type=MESH)
 
-    partners = [peer] + [at_chip(d * sign) for d in range(1, REACH + 1) for sign in (1, -1)]
-    for partner in partners:
-        pl.semaphore_signal(barrier, inc=1, device_id=partner, device_id_type=MESH)
-    for copy in field_loads + cond_loads + small_loads + prof_loads:
+    for copy in field_loads + cond_loads + small_loads:
         copy.start()
 
     sends = []
@@ -156,6 +160,10 @@
 
     edges = lax.min(xy, 1) + lax.min(n_xy - 1 - xy, 1)
     pl.semaphore_wait(barrier, len(partners) + edges)
+    for sign in (1, -1):
+        pl.semaphore_signal(
+            near_sem, inc=1, device_id=at_chip(sign * (REACH - KNOWN)), device_id_type=MESH
+        )
     to_left = describe(halo_s.at[0], halo_r.at[1], left)
     to_right = describe(halo_s.at[1], halo_r.at[0], right)
     sides = ((has_left, to_left, to_right, 0), (has_right, to_right, to_left, 1))
@@ -164,6 +172,8 @@
         def _(outward=outward):
             outward.start()
 
+    for copy in prof_loads:
+        copy.start()
     pair_c = remote(pair_cs, blk_c.at[core], peer)
 
     @pl.loop(0, 16, unroll=4)
@@ -214,7 +224,17 @@
         for n in range(3):
             chip_coef[i, n] = held[n]
             target[i, n] = merged[n]
-    ring_c = [remote(ring_cs.at[i], ring_cr.at[i], at_chip(TO[i])) for i in SENT]
+    def send_mass(far):
+        return [
+            remote(ring_cs.at[i], ring_cr.at[i], at_chip(TO[i]))
+            for i in SENT
+            if (abs(TO[i]) > KNOWN) == far
+        ]
+
+    ring_c = send_mass(False)
+    pl.semaphore_wait(near_sem, 2)
+    ring_c += send_mass(True)
+
 
     for copy in small_loads:
         copy.wait()
@@ -260,31 +280,34 @@
                 )
         return block
 
-    @pl.loop(0, 16, unroll=4)
-    def _(p):
-        block = eliminate_rhs(other, p)
+    pair_r = []
+    for begin, end in OUT:
+        for k in range(begin, end):
+            block = eliminate_rhs(other, part_at(PLACES[k]))
+            for n in range(2):
+                pair_rs[k, n] = block[n]
+        piece = pl.ds(begin, end - begin)
+        pair_r.append(remote(pair_rs.at[piece], blk_r.at[core, piece], peer))
+    for k in range(CHIPS):
+        block = eliminate_rhs(core, part_at(PLACES[k]))
         for n in range(2):
-            pair_rs[p, n] = block[n]
-
-    pair_r = remote(pair_rs, blk_r.at[core], peer)
-
-    @pl.loop(0, 16, unroll=4)
-    def _(p):
-        block = eliminate_rhs(core, p)
-        for n in range(2):
-            blk_r[core, p, n] = block[n]
-
-    pair_r.wait_recv()
-    for i in range(CHIPS):
-        p = part_at(i)
-        merged, chip_coef[i, 2] = merge_rhs(
-            *([blk_r[c, p, n] for n in range(2)] for c in range(2)),
-            *(chip_coef[i, n] for n in range(3)),
-        )
-        target = ring_rs if TO[i] else ring_rr
-        for n in range(2):
-            target[i, n] = merged[n]
-    ring_r = [remote(ring_rs.at[i], ring_rr.at[i], at_chip(TO[i])) for i in SENT]
+            blk_r[core, k, n] = block[n]
+
+    ring_r = []
+    for copy, (begin, end) in zip(pair_r, OUT):
+        copy.wait_recv()
+        for k in range(begin, end):
+            i = PLACES[k]
+            merged, chip_coef[i, 2] = merge_rhs(
+                *([blk_r[c, k, n] for n in range(2)] for c in range(2)),
+                *(chip_coef[i, n] for n in range(3)),
+            )
+            target = ring_rs if TO[i] else ring_rr
+            for n in range(2):
+                target[i, n] = merged[n]
+        for i in PLACES[begin:end]:
+            if TO[i]:
+                ring_r.append(remote(ring_rs.at[i], ring_rr.at[i], at_chip(TO[i])))
 
     for j in range(3):
         powers(j)
@@ -415,7 +438,7 @@
             target = ret_s if TO[i] else ret_r
             for n in range(2):
                 target[i, n] = values[b + n]
-    ret = [remote(ret_s.at[i], ret_r.at[i], at_chip(-TO[i])) for i in SENT]
+    ret = {i: remote(ret_s.at[i], ret_r.at[i], at_chip(-TO[i])) for i in SENT}
 
     evolve(1)
     evolve(2)
@@ -434,18 +457,6 @@
         delta[j] = spreads[:, 128 * j : 128 * j + 128]
     delta[3] = jnp.zeros((256, 128), F32)
 
-    for copy in ret:
-        copy.wait_recv()
-    for i in range(CHIPS):
-        p = part_at(i)
-        low, high = ret_r[i, 0], ret_r[i, 1]
-        middle = chip_coef[i, 2] + chip_coef[i, 0] * low + chip_coef[i, 1] * high
-        fin[0, p, 0] = low
-        fin[0, p, 1] = middle
-        fin[1, p, 0] = middle
-        fin[1, p, 1] = high
-    last = remote(fin.at[other], fin_r, peer)
-
     def finish(owner, p, low, high):
         f, y = owner * 2 + p // 8, lax.rem(p, 8)
         e = owner * 16 + p
@@ -459,16 +470,27 @@
             at = pl.ds(pl.multiple_of(f * 32 + z * 8, 8), 8)
             out_fields[at, lanes] = values[z] + delta[f, pl.ds(pl.multiple_of(z * 64 + y * 8, 8), 8), :]
 
-    @pl.loop(0, 16, unroll=4)
-    def _(p):
-        finish(core, p, fin[core, p, 0], fin[core, p, 1])
-
-    last.wait_recv()
-
-    @pl.loop(0, 16, unroll=4)
-    def _(p):
-        finish(other, p, fin_r[p, 0], fin_r[p, 1])
-
+    last = []
+    for begin, end in BACK:
+        for i in PLACES[begin:end]:
+            if TO[i]:
+                ret[i].wait_recv()
+        for k in range(begin, end):
+            i = PLACES[k]
+            low, high = ret_r[i, 0], ret_r[i, 1]
+            middle = chip_coef[i, 2] + chip_coef[i, 0] * low + chip_coef[i, 1] * high
+            fin[0, k, 0] = low
+            fin[0, k, 1] = middle
+            fin[1, k, 0] = middle
+            fin[1, k, 1] = high
+        piece = pl.ds(begin, end - begin)
+        last.append(remote(fin.at[other, piece], fin_r.at[piece], peer))
+        for k in range(begin, end):
+            finish(core, part_at(PLACES[k]), fin[core, k, 0], fin[core, k, 1])
+    for copy, (begin, end) in zip(last, BACK):
+        copy.wait_recv()
+        for k in range(begin, end):
+            finish(other, part_at(PLACES[k]), fin_r[k, 0], fin_r[k, 1])
     for present, outward, unused, unused_side in sides:
         @pl.when(present)
         def _(outward=outward):
@@ -528,8 +550,9 @@
             pltpu.SemaphoreType.DMA((16,)),
             pltpu.SemaphoreType.DMA((5,)),
             pltpu.SemaphoreType.DMA((3,)),
-            pltpu.SemaphoreType.DMA((51,)),
-            pltpu.SemaphoreType.DMA((51,)),
+            pltpu.SemaphoreType.DMA((56,)),
+            pltpu.SemaphoreType.DMA((56,)),
+            pltpu.SemaphoreType.REGULAR,
         ],
         compiler_params=pltpu.CompilerParams(
             collective_id=0, has_side_effects=True, vmem_limit_bytes=40 * 2**20

time: 42.8 us -> 41.4 us (0.967)
  Pallas kernels: 41.4 us -> 39.9 us
    pallas_call x1, Pallas kernels: 40 us -> 38.5 us  [body(): pl.pallas_call(functools.partial(kernel, lax.axis_size('xy')), out_shape=...]
where the time goes in v4:
time: 41.4 us; the launch traced here: 41.2 us
  Pallas kernels  39.9 us (96%)
  between operations  1.29 us (3%)
    pallas_call x1, Pallas kernels, body(): pl.pallas_call(functools.partial(kernel, lax.axis_size('xy')), out_shape=...  38.5 us
    pallas_call x1, Pallas kernels, body(): pl.pallas_call(deliver, out_shape=(pltpu.HBM((128, 1024), F32), pltpu.HBM...  1.38 us

profile of v4, /device:TPU:1, one launch (start us, length us, event | category | flops | bytes accessed | tf_op | source)
XLA Modules:
  0.0 41.2 jit_solution(4767052048461863585)
XLA Ops:
  1.3 38.5 %ingot.1 = (f32[128,1024]{1,0:T(8,128)S(1)}, f32[3072,128]{1,0:T(8,128)S(1)}) custom-call(f32[128,1024]{1,0:T(8,128)} %bitcast.7, f32[128,1024]{1,0:T(8,128)} %bitcast.8, f32[4]{0:T(128)} %lateral_in.1, f32[3]{0:T(128)} %partition_in.1, f32[3,64,64]{2,1,0:T(8,128)} %arm_in.1, f32[3072,128]{1,0:T(8,128)} %bitcast.5, s32[1,16]{1,0:T(1,128)} %ids_in.1, ...), custom_call_target="tpu_custom_call" | custom-call | flops 1000000000 | bytes 5242880 | tf_op jit(solution)/shard_map/ingot/pallas_call | solution.py:538
  39.8 1.4 %deliver.1 = (f32[128,1024]{1,0:T(8,128)}, f32[3072,128]{1,0:T(8,128)}) custom-call(f32[128,1024]{1,0:T(8,128)S(1)} %get-tuple-element.6.new_fields, f32[3072,128]{1,0:T(8,128)S(1)} %get-tuple-element.7.new_profiles), custom_call_target="tpu_custom_call" | custom-call | bytes 4194304 | tf_op jit(solution)/shard_map/deliver/pallas_call | solution.py:563

commit v5 on v4

--- a/solution.py
+++ b/solution.py
@@ -21,7 +21,7 @@
 TO = [REACH - i for i in range(HALF)] + [2 * REACH - i for i in range(HALF, CHIPS)]
 PLACES = sorted(range(CHIPS), key=lambda i: (-abs(TO[i]), i))
 SENT = PLACES[:-2]
-OUT = ((0, 4), (4, 8), (8, 12), (12, 16))
+OUT = ((0, 6), (6, 16))
 BACK = ((10, 16), (4, 10), (0, 4))
 
 
@@ -172,8 +172,6 @@
         def _(outward=outward):
             outward.start()
 
-    for copy in prof_loads:
-        copy.start()
     pair_c = remote(pair_cs, blk_c.at[core], peer)
 
     @pl.loop(0, 16, unroll=4)
@@ -235,6 +233,9 @@
     pl.semaphore_wait(near_sem, 2)
     ring_c += send_mass(True)
 
+
+    for copy in prof_loads:
+        copy.start()
 
     for copy in small_loads:
         copy.wait()

time: 41.4 us -> 41.3 us (level)
  no operation moved by 1% of the time
where the time goes in v5:
time: 41.3 us; the launch traced here: 41.2 us
  Pallas kernels  39.9 us (97%)
  between operations  1.29 us (3%)
    pallas_call x1, Pallas kernels, body(): pl.pallas_call(functools.partial(kernel, lax.axis_size('xy')), out_shape=...  38.5 us
    pallas_call x1, Pallas kernels, body(): pl.pallas_call(deliver, out_shape=(pltpu.HBM((128, 1024), F32), pltpu.HBM...  1.38 us

profile of v5, /device:TPU:1, one launch (start us, length us, event | category | flops | bytes accessed | tf_op | source)
XLA Modules:
  0.0 41.2 jit_solution(15376555951564132256)
XLA Ops:
  1.3 38.5 %ingot.1 = (f32[128,1024]{1,0:T(8,128)S(1)}, f32[3072,128]{1,0:T(8,128)S(1)}) custom-call(f32[128,1024]{1,0:T(8,128)} %bitcast.7, f32[128,1024]{1,0:T(8,128)} %bitcast.8, f32[4]{0:T(128)} %lateral_in.1, f32[3]{0:T(128)} %partition_in.1, f32[3,64,64]{2,1,0:T(8,128)} %arm_in.1, f32[3072,128]{1,0:T(8,128)} %bitcast.5, s32[1,16]{1,0:T(1,128)} %ids_in.1, ...), custom_call_target="tpu_custom_call" | custom-call | flops 1000000000 | bytes 5242880 | tf_op jit(solution)/shard_map/ingot/pallas_call | solution.py:539
  39.8 1.4 %deliver.1 = (f32[128,1024]{1,0:T(8,128)}, f32[3072,128]{1,0:T(8,128)}) custom-call(f32[128,1024]{1,0:T(8,128)S(1)} %get-tuple-element.6.new_fields, f32[3072,128]{1,0:T(8,128)S(1)} %get-tuple-element.7.new_profiles), custom_call_target="tpu_custom_call" | custom-call | bytes 4194304 | tf_op jit(solution)/shard_map/deliver/pallas_call | solution.py:564
